TPU v7x, 32 devices: a whole 2x2x4 slice. The times are simulated.
32 devices in a mesh: seq: 2 (over core), head: 4 (over z), dp: 4 (over y, x).
Axes of the slice: x: 2, y: 2, z: 4, core: 2. Of those that a mesh axis runs over, the one named last changes fastest.
Arguments:
- tokens: bfloat16 [4, 256, 4096], P('dp', 'seq', 'head'), may hold values from -6 to 6
- w_qkv: bfloat16 [4096, 3, 512], P(('seq', 'dp'), None, 'head'), may hold values from -0.09375 to 0.09375
- w_lr: bfloat16 [4096, 4], P(None, 'head'), may hold values from -0.1875 to 0.1875
- w_out: bfloat16 [4096, 512], P(('seq', 'dp'), 'head'), may hold values from -0.25 to 0.25
- w1_init: float32 [4, 128, 512], P('head'), may hold values from -0.5 to 0.5
- w2_init: float32 [4, 512, 128], P('head'), may hold values from -0.25 to 0.25
- d_out: bfloat16 [4, 256, 4096], P('dp', 'seq', 'head'), may hold values from -6 to 6
Outputs:
- out: bfloat16 [4, 256, 4096], P('dp', 'seq', 'head')
- d_tokens: bfloat16 [4, 256, 4096], P('dp', 'seq', 'head')
- d_w1_init: float32 [4, 128, 512], P('head', None, ('seq', 'dp'))
- d_w2_init: float32 [4, 512, 128], P('head', ('seq', 'dp'))
All inputs are finite; a program needn't handle non-finite values.
Results may differ from a plain program's by a relative error of at most 0.018.
Values may be sent and summed in bfloat16 or wider, within the bound.
No kernel may reach another device: no remote copies, remote signals or barrier semaphores. Data moves between devices by JAX's collectives and lax.ppermute only.
A program may use at most 64 MiB of HBM per device.

v0:
```python
import functools

import jax
import jax.numpy as jnp
from jax import lax
from jax.experimental import pallas as pl
from jax.experimental.pallas import tpu as pltpu
from jax.sharding import PartitionSpec as P

MB = 64
EPSILON = 1e-06
BASE_RATE = 0.1
GELU_SCALE = 0.7978845608028654
GELU_CUBIC = 0.044715
NN = ((1,), (0,))
NT = ((1,), (1,))
TN = ((0,), (0,))
EXTRA = 16
UNROLL_LIMIT = 8
F32 = jnp.float32
BF16 = jnp.bfloat16


def mm(left, right, dims):
    return lax.dot_general(
        left.astype(BF16), right.astype(BF16), (dims, ((), ())), preferred_element_type=F32
    )


def padded(lines):
    return jnp.concatenate([lines, jnp.zeros_like(lines)], axis=1)


def mean(rows):
    return jnp.mean(rows, axis=-1, keepdims=True)


def gelu_parts(v):
    square = v * v
    bend = jnp.tanh(v * (GELU_SCALE + (GELU_SCALE * GELU_CUBIC) * square))
    half = 0.5 + 0.5 * bend
    slope = GELU_SCALE + (3.0 * GELU_SCALE * GELU_CUBIC) * square
    bell = 0.5 - 0.5 * bend * bend
    lean = bell * slope
    second = 2.0 * lean * (1.0 - v * bend * slope) + (6.0 * GELU_SCALE * GELU_CUBIC) * square * bell
    return v * half, half + v * lean, second


def gelu_two(v):
    square = v * v
    bend = jnp.tanh(v * (GELU_SCALE + (GELU_SCALE * GELU_CUBIC) * square))
    half = 0.5 + 0.5 * bend
    slope = GELU_SCALE + (3.0 * GELU_SCALE * GELU_CUBIC) * square
    return v * half, half + v * ((0.5 - 0.5 * bend * bend) * slope)


def mate(index, step, count):
    if count & (count - 1) == 0:
        return index ^ step
    return (index + step) % count


def hop(array, axis, step):
    count = lax.axis_size(axis)
    return lax.ppermute(array, axis, [(mate(i, step, count), i) for i in range(count)])


def peers_of(array, axis):
    return [array] + [hop(array, axis, j) for j in range(1, lax.axis_size(axis))]


def sent_to(arrays, axis):
    count = lax.axis_size(axis)
    back = [arrays[0]]
    for j in range(1, count):
        back.append(lax.ppermute(arrays[j], axis, [(i, mate(i, j, count)) for i in range(count)]))
    return back


def in_plane(array, forward):
    if lax.axis_size("dp") == 4:
        near = [array, hop(array, "dp", 1), hop(array, "dp", 2)]
        near.append(hop(near[forward], "dp", 3 - forward) if forward else hop(array, "dp", 3))
    else:
        near = peers_of(array, "dp")
    columns = [peers_of(piece, "seq") for piece in near]
    return [list(pieces) for pieces in zip(*columns)]


def owner_of(place_ref, seqs, dps, share, j, d):
    seq, dp = place_ref[0], place_ref[2]
    k = mate(seq, j, seqs) * dps + mate(dp, d, dps)
    return k // share, k % share


def rate_line(block, depth):
    rows = block.astype(F32)
    return jnp.concatenate([rows[i : i + 1, :] for i in range(depth // 128)], axis=1)


def outer_kernel(seqs, heads, dps, share, place_ref, tok_ref, dout_ref, *refs):
    w_refs = refs[: seqs * dps]
    out_refs = refs[seqs * dps : seqs * dps + heads]
    tok_s, dout_s, acc = refs[seqs * dps + heads :]
    rows, features = tok_ref.shape
    depth = features // share
    for r in range(share):
        tok_s[r] = tok_ref[:, r * depth : (r + 1) * depth]
        dout_s[r] = dout_ref[:, r * depth : (r + 1) * depth]
    acc[...] = jnp.zeros_like(acc)
    for j in range(seqs):
        for d in range(dps):
            w = w_refs[j * dps + d]
            h, r = owner_of(place_ref, seqs, dps, share, j, d)
            line = rate_line(w[depth:, :], depth)
            logit = mm(jnp.broadcast_to(line, (EXTRA, depth)), tok_s[r], NT)
            back = mm(dout_s[r], w[0:depth, :], NN)
            acc[h] = acc[h] + jnp.concatenate([back, logit], axis=0)
    first_half = lax.broadcasted_iota(jnp.int32, (EXTRA, rows), 0) < EXTRA // 2
    for j in range(heads):
        total = acc[mate(place_ref[1], j, heads)]
        out_refs[j][0:rows, :] = total[0:rows].astype(BF16)
        logit = total[rows:]
        high = logit.astype(BF16).astype(F32)
        out_refs[j][rows:, :] = jnp.where(first_half, high, logit - high).astype(BF16)


def inner_projection_kernel(seqs, heads, dps, share, place_ref, tok_ref, *refs):
    w_refs = refs[: 2 * seqs * dps]
    out_refs = refs[2 * seqs * dps : 2 * seqs * dps + heads]
    tok_s, acc = refs[2 * seqs * dps + heads :]
    rows, features = tok_ref.shape
    depth = features // share
    half = depth // 2
    for r in range(share):
        tok_s[r] = tok_ref[:, r * depth : (r + 1) * depth]
    acc[...] = jnp.zeros_like(acc)
    for part in range(2):
        for j in range(seqs):
            for d in range(dps):
                w = w_refs[(part * seqs + j) * dps + d]
                h, r = owner_of(place_ref, seqs, dps, share, j, d)
                wide = jnp.concatenate([w[c * half : (c + 1) * half, :] for c in range(3)], axis=1)
                acc[h] = acc[h] + mm(tok_s[r][:, part * half : (part + 1) * half], wide, NN)
    for j in range(heads):
        out_refs[j][...] = acc[mate(place_ref[1], j, heads)].astype(BF16)


def inner_kernel(seqs, dps, place_ref, *refs):
    x_refs, y_refs = refs[:seqs], refs[seqs : 2 * seqs]
    w1_ref, w2_ref, res_ref = refs[2 * seqs : 2 * seqs + 3]
    dw_refs = refs[2 * seqs + 3 : 2 * seqs + 3 + dps]
    (
        qs, ks, vs, ds, es, sg, os, lg,
        w1c, w2c, w1b, w2b,
        x2s, g1s, pgs, gfs, xqs, zqs, dx2s, dg1s,
        dys, ns, rs, ss, cs, g2s, dg2s, dks, des, ws,
    ) = refs[2 * seqs + 3 + dps :]
    rows = x_refs[0].shape[0]
    hd = y_refs[0].shape[1]
    width = 4 * hd
    blocks = seqs * rows // MB
    per = rows // MB
    place = place_ref[0]

    for j in range(seqs):
        owner = mate(place, j, seqs)
        at = pl.ds(pl.multiple_of(owner * rows, rows), rows)
        qs[at, :] = x_refs[j][:, 0:hd]
        ks[at, :] = x_refs[j][:, hd : 2 * hd]
        vs[at, :] = x_refs[j][:, 2 * hd : 3 * hd]
        ds[at, :] = y_refs[j][0:rows, :]
        logit = y_refs[j][rows : rows + 8, :] + y_refs[j][rows + 8 : rows + 16, :]
        gate = jax.nn.sigmoid(logit)
        scaled = (BASE_RATE / hd) * gate
        for b in range(per):
            es[owner * per + b] = padded(scaled[:, b * MB : (b + 1) * MB])
            sg[owner * per + b] = padded((scaled * (1.0 - gate))[:, b * MB : (b + 1) * MB])

    w1c[...] = w1_ref[...]
    start = w2_ref[...]
    w2c[...] = (start - mean(start)).T

    at_row = lax.broadcasted_iota(jnp.int32, (MB, MB), 0)
    at_col = lax.broadcasted_iota(jnp.int32, (MB, MB), 1)
    causal = at_col <= at_row
    diagonal = at_col == at_row

    def to_column(line):
        return jnp.sum(jnp.where(diagonal, line, 0.0), axis=1, keepdims=True)

    def to_line(column):
        return jnp.sum(jnp.where(diagonal, column, 0.0), axis=0, keepdims=True)

    def at_block(i):
        if isinstance(i, int):
            return slice(i * MB, (i + 1) * MB)
        return pl.ds(pl.multiple_of(i * MB, MB), MB)

    def forward(i):
        at = at_block(i)
        q, k, v, d_o = qs[at, :], ks[at, :], vs[at, :], ds[at, :]
        line = es[i][0:1, 0:MB]
        e = to_column(line)
        mask = jnp.where(causal, line, 0.0)
        w1 = w1c[...].astype(BF16)
        w2 = w2c[...].astype(BF16)
        w1b[i] = w1
        w2b[i] = w2
        kb, qb = k.astype(BF16), q.astype(BF16)
        gap = v - k
        gap = gap - mean(gap)
        both = mm(jnp.concatenate([kb, qb], axis=0), w1, NN)
        x2, g1, gg1 = gelu_parts(both[:MB])
        x2b = x2.astype(BF16)
        c = mm(x2b, w2, NT)
        var = mean(c * c)
        cross = mean(gap * c)
        s = lax.rsqrt(var + EPSILON)
        n = c * s
        cc = var * s * s - s * cross
        r = n - gap
        g2 = s * (r - n * cc)
        g2b = g2.astype(BF16)
        p = mm(g2b, w2, NN)
        g1f = p * g1
        w1c[...] = w1c[...] - mm(k, e * g1f, TN)
        w2c[...] = w2c[...] - mm(e * g2, x2b, TN)
        g1b = g1f.astype(BF16)
        b1 = mm(qb, kb, NT)
        a1 = (b1 * mask).astype(BF16)
        zq = both[MB:] - mm(a1, g1b, NN)
        xq, gq = gelu_two(zq)
        xqb = xq.astype(BF16)
        b2 = mm(xqb, x2b, NT)
        a2 = (b2 * mask).astype(BF16)
        y = mm(xqb, w2, NT) - mm(a2, g2b, NN)
        sq = lax.rsqrt(mean(y * y) + EPSILON)
        nq = y * sq
        os[at, 3 * hd : 4 * hd] = (q + nq).astype(BF16)
        dy = sq * (d_o - mean(d_o) - nq * mean(d_o * nq))
        dyb = dy.astype(BF16)
        da2 = -mm(dyb, g2b, NT)
        db2 = (da2 * mask).astype(BF16)
        dg2s[i] = -mm(a2, dyb, TN)
        dxq = mm(dyb, w2, NN) + mm(db2, x2b, NN)
        dx2s[i] = mm(db2, xqb, TN)
        dzq = (dxq * gq).astype(BF16)
        da1 = -mm(dzq, g1b, NT)
        db1 = (da1 * mask).astype(BF16)
        dg1s[i] = -mm(a1, dzq, TN)
        dq = d_o + mm(dzq, w1, NT) + mm(db1, kb, NN)
        os[at, 0:hd] = dq.astype(BF16)
        dks[i] = mm(db1, qb, TN)
        de = jnp.sum(jnp.where(causal, da2 * b2 + da1 * b1, 0.0), axis=0, keepdims=True)
        des[i] = padded(jnp.broadcast_to(de, (8, MB)))
        x2s[i] = x2b
        g1s[i] = g1
        pgs[i] = p * gg1
        gfs[i] = g1f
        xqs[i] = xqb
        zqs[i] = dzq
        dys[i] = dyb
        ns[i] = n
        rs[i] = r
        ss[i] = jnp.broadcast_to(s, (MB, hd))
        cs[i] = jnp.broadcast_to(cc, (MB, hd))
        g2s[i] = g2

    def backward(i):
        at = at_block(i)
        q, k = qs[at, :], ks[at, :]
        e = to_column(es[i][0:1, 0:MB])
        w1, w2 = w1b[i], w2b[i]
        d1, d2 = w1c[...].astype(BF16), w2c[...].astype(BF16)
        x2b, g1, g1f, g2 = x2s[i], g1s[i], gfs[i], g2s[i]
        n, s, cc = ns[i], ss[i], cs[i]
        dh1 = -mm(k, d1, NN)
        dh2 = -mm(x2b, d2, NT)
        dg1 = dg1s[i] + e * dh1
        dp = (dg1 * g1).astype(BF16)
        dg2 = dg2s[i] + e * dh2 + mm(dp, w2, NT)
        dt = s * dg2
        mt = mean(dt * n)
        dr = dt - mean(dt) - n * mt
        dn = dr - cc * dt - rs[i] * mt
        du = s * (dn - mean(dn) - n * (mean(dn * n) + mean(dg2 * g2)))
        dub = du.astype(BF16)
        mixed = jnp.concatenate([(-e * g2).astype(BF16), dub], axis=1)
        dx2 = dx2s[i] + mm(mixed, jnp.concatenate([d2, w2], axis=0), NN)
        dz1 = (dg1 * pgs[i] + dx2 * g1).astype(BF16)
        mixed = jnp.concatenate([(-e * g1f).astype(BF16), dz1], axis=1)
        dk = dks[i] + dr + mm(mixed, jnp.concatenate([d1, w1], axis=1), NT)
        w1c[...] = w1c[...] + mm(
            jnp.concatenate([q, k], axis=0), jnp.concatenate([zqs[i], dz1], axis=0), TN
        )
        w2c[...] = w2c[...] + mm(
            jnp.concatenate([dys[i].astype(F32), du, g2], axis=0),
            jnp.concatenate([xqs[i], x2b, dp], axis=0),
            TN,
        )
        extra = jnp.sum(g1f * dh1, axis=1, keepdims=True) + jnp.sum(
            g2 * dh2, axis=1, keepdims=True
        )
        line = (des[i][0:1, 0:MB] + to_line(extra)) * sg[i][0:1, 0:MB]
        lg[i] = padded(jnp.broadcast_to(line, (8, MB)))
        os[at, hd : 2 * hd] = dk.astype(BF16)
        os[at, 2 * hd : 3 * hd] = (-dr).astype(BF16)

    def loop(step, order):
        if blocks <= UNROLL_LIMIT:
            for i in range(blocks):
                step(order(i))
        else:
            lax.fori_loop(0, blocks, lambda i, unused: (step(order(i)), unused)[1], 0)

    loop(forward, lambda i: i)
    w1c[...] = jnp.zeros_like(w1c)
    w2c[...] = jnp.zeros_like(w2c)
    loop(backward, lambda i: blocks - 1 - i)

    res_ref[0:rows, :] = os[pl.ds(pl.multiple_of(place * rows, rows), rows), :]
    res_ref[rows:, :] = jnp.zeros((EXTRA, width), BF16)
    first_row = lax.broadcasted_iota(jnp.int32, (EXTRA, rows), 0) == 0
    lines = jnp.concatenate([lg[place * per + b][0:1, 0:MB] for b in range(per)], axis=1)
    lines = jnp.where(first_row, jnp.broadcast_to(lines, (EXTRA, rows)), 0.0)
    res_ref[rows:, 0:rows] = lines.astype(BF16)

    part = dw_refs[0].shape[0]
    ws[:, 0:hd] = w1c[...].T
    ws[:, hd : 2 * hd] = w2c[...].T
    for d in range(dps):
        first = (place * dps + mate(place_ref[2], d, dps)) * part
        dw_refs[d][...] = ws[pl.ds(pl.multiple_of(first, part), part), :]


def output_kernel(seqs, heads, dps, share, place_ref, *refs):
    got_refs, refs = refs[:heads], refs[heads:]
    o_refs, w_refs = refs[: seqs * dps], refs[seqs * dps : 3 * seqs * dps]
    out_ref, dtok_ref, got, out_s, grad_s = refs[3 * seqs * dps :]
    hd = o_refs[0].shape[1]
    rows, features = out_ref.shape
    depth = features // share
    half = depth // 2
    for j in range(heads):
        got[mate(place_ref[1], j, heads)] = got_refs[j][...]
    out_s[...] = jnp.zeros_like(out_s)
    grad_s[...] = jnp.zeros_like(grad_s)
    for j in range(seqs):
        for d in range(dps):
            o = o_refs[j * dps + d]
            h, r = owner_of(place_ref, seqs, dps, share, j, d)
            out_s[r] = out_s[r] + mm(got[h, 0:rows, 3 * hd :], o[0:depth, :], NT)
            line = rate_line(o[depth:, :], depth)
            logit = got[h, rows:, 0:rows].astype(F32).T
            grad = [mm(logit, jnp.broadcast_to(line, (EXTRA, depth)), NN)]
            mine = got[h, 0:rows, 0 : 3 * hd]
            halves = []
            for part in range(2):
                w = w_refs[(part * seqs + j) * dps + d]
                wide = jnp.concatenate([w[c * half : (c + 1) * half, :] for c in range(3)], axis=1)
                halves.append(mm(mine, wide, NT))
            grad_s[r] = grad_s[r] + grad[0] + jnp.concatenate(halves, axis=1)
    for r in range(share):
        out_ref[:, r * depth : (r + 1) * depth] = out_s[r].astype(BF16)
        dtok_ref[:, r * depth : (r + 1) * depth] = grad_s[r].astype(BF16)


VMEM = pl.BlockSpec(memory_space=pltpu.VMEM)
SMEM = pl.BlockSpec(memory_space=pltpu.SMEM)
PARAMS = pltpu.CompilerParams(vmem_limit_bytes=48 * 1024 * 1024)


def call(kernel, outs, operands, scratch=()):
    return pl.pallas_call(
        kernel,
        out_shape=outs,
        in_specs=[SMEM] + [VMEM] * (len(operands) - 1),
        out_specs=jax.tree.map(lambda unused: VMEM, outs),
        scratch_shapes=list(scratch),
        compiler_params=PARAMS,
    )(*operands)


def body(tokens, w_qkv, w_lr, w_out, w1_init, w2_init, d_out):
    seqs, heads, dps = (lax.axis_size(a) for a in ("seq", "head", "dp"))
    share = seqs * dps // heads
    rows, features = tokens.shape[1:]
    depth, unused, hd = w_qkv.shape
    inner = w1_init.shape[2]
    blocks = seqs * rows // MB
    place = jnp.stack([lax.axis_index(a).astype(jnp.int32) for a in ("seq", "head", "dp")])
    sizes = (seqs, heads, dps, share)

    pairs = []
    for seq in range(seqs):
        for head in range(heads):
            for dp in range(dps):
                k = seq * dps + dp
                target = head * share + k % share
                to = ((target // dps) * heads + k // share) * dps + target % dps
                pairs.append(((seq * heads + head) * dps + dp, to))

    def swapped(array):
        return lax.ppermute(array, ("seq", "head", "dp"), pairs)

    half = depth // 2
    lines = w_lr[:, 0].reshape(seqs * dps, depth // 128, 128)
    line = lax.dynamic_index_in_dim(
        lines, lax.axis_index("seq") * dps + lax.axis_index("dp"), 0, keepdims=False
    )
    line = jnp.pad(line, ((0, EXTRA - depth // 128), (0, 0)))
    outer_w = swapped(jnp.concatenate([w_out, line], axis=0))
    by_kind = w_qkv.transpose(1, 0, 2)
    first_w = swapped(by_kind[:, :half].reshape(3 * half, hd))
    second = by_kind[:, half:].reshape(3 * half, hd)
    second, first_w, outer_w = lax.optimization_barrier((second, first_w, outer_w))
    second_w = swapped(second)
    outer_ws = sum(in_plane(outer_w, 0), [])
    inner_ws = sum(in_plane(first_w, 1), []) + sum(in_plane(second_w, 2), [])

    def summed(arrays):
        return functools.reduce(lambda a, b: a + b, [a.astype(F32) for a in arrays])

    outer_part = call(
        functools.partial(outer_kernel, *sizes),
        (jax.ShapeDtypeStruct((rows + EXTRA, hd), BF16),) * heads,
        (place, tokens[0], d_out[0], *outer_ws),
        [pltpu.VMEM((share, rows, features // share), BF16)] * 2
        + [pltpu.VMEM((heads, rows + EXTRA, hd), F32)],
    )
    outer_all = peers_of(summed(sent_to(outer_part, "head")), "seq")
    later_place, unused = lax.optimization_barrier((place, outer_part[0]))
    inner_part = call(
        functools.partial(inner_projection_kernel, *sizes),
        (jax.ShapeDtypeStruct((rows, 3 * hd), BF16),) * heads,
        (later_place, tokens[0], *inner_ws),
        [
            pltpu.VMEM((share, rows, features // share), BF16),
            pltpu.VMEM((heads, rows, 3 * hd), F32),
        ],
    )
    inner_all = peers_of(summed(sent_to(inner_part, "head")), "seq")

    long = seqs * rows
    scratch = (
        [pltpu.VMEM((long, hd), F32)] * 4
        + [pltpu.VMEM((blocks, 8, 2 * MB), F32)] * 2
        + [pltpu.VMEM((long, 4 * hd), BF16), pltpu.VMEM((blocks, 8, 2 * MB), F32)]
        + [pltpu.VMEM((hd, inner), F32)] * 2
        + [pltpu.VMEM((blocks, hd, inner), BF16)] * 2
        + [pltpu.VMEM((blocks, MB, inner), t) for t in (BF16, F32, F32, F32, BF16, BF16, F32, F32)]
        + [pltpu.VMEM((blocks, MB, hd), t) for t in (BF16, F32, F32, F32, F32, F32, F32, F32)]
        + [pltpu.VMEM((blocks, 8, 2 * MB), F32), pltpu.VMEM((inner, 2 * hd), F32)]
    )
    part = inner // (seqs * dps)
    result, *d_inner = call(
        functools.partial(inner_kernel, seqs, dps),
        (jax.ShapeDtypeStruct((rows + EXTRA, 4 * hd), BF16),)
        + (jax.ShapeDtypeStruct((part, 2 * hd), F32),) * dps,
        (place, *inner_all, *outer_all, w1_init[0], w2_init[0]),
        scratch,
    )
    got = peers_of(result, "head")
    unused, *d_inner = lax.optimization_barrier((got[1], *d_inner))
    shares = summed(sent_to(d_inner, "dp"))
    out, d_tokens = call(
        functools.partial(output_kernel, *sizes),
        (jax.ShapeDtypeStruct((rows, features), BF16),) * 2,
        (place, *got, *outer_ws, *inner_ws),
        [
            pltpu.VMEM((heads, rows + EXTRA, 4 * hd), BF16),
            pltpu.VMEM((share, rows, features // share), F32),
            pltpu.VMEM((share, rows, features // share), F32),
        ],
    )
    return (out[None], d_tokens[None], shares[:, :hd].transpose(1, 0)[None], shares[:, hd:][None])


def solution(mesh):
    placed = (
        P("dp", "seq", "head"),
        P(("seq", "dp"), None, "head"),
        P(None, "head"),
        P(("seq", "dp"), "head"),
        P("head", None, None),
        P("head", None, None),
        P("dp", "seq", "head"),
    )
    return jax.shard_map(
        body,
        mesh=mesh,
        in_specs=placed,
        out_specs=(
            P("dp", "seq", "head"),
            P("dp", "seq", "head"),
            P("head", None, ("seq", "dp")),
            P("head", ("seq", "dp"), None),
        ),
        check_vma=False,
    )
```

profile of v0, /device:TPU:0, one launch (start us, length us, event | category | flops | bytes accessed | tf_op | source)
XLA Modules:
  0.0 111.6 jit_solution(6393232646793281331)
XLA Ops:
  0.7 1.1 fusion.2
  1.8 0.8 collective-permute-start
  2.7 0.7 collective-permute-start.1
  3.4 3.0 %collective-permute-start.2 = (bf16[528,128]{1,0:T(8,128)(2,1)S(1)}, bf16[528,128]{1,0:T(8,128)(2,1)S(1)}, u32[]{:S(2)}, u32[]{:S(2)}) collective-permute-start(bf16[528,128]{1,0:T(8,128)(2,1)S(1)} %collective-permute-done.1.refs_0_.refs_4_), channel_id=1, source_target_pairs={{1,0},{0,1},{3,2},{2,3},{5,4},{4,5},{7,6},{6,7},{9,8},{8,9},{11,10... | collective-permute-start | bytes 405512 | tf_op jit(solution)/shard_map/ppermute | solution.py:65
  6.4 16.6 %collective-permute-start.3 = (bf16[528,128]{1,0:T(8,128)(2,1)S(1)}, bf16[528,128]{1,0:T(8,128)(2,1)S(1)}, u32[]{:S(2)}, u32[]{:S(2)}) collective-permute-start(bf16[528,128]{1,0:T(8,128)(2,1)S(1)} %collective-permute-done.1.refs_0_.refs_4_), channel_id=1, source_target_pairs={{2,0},{3,1},{0,2},{1,3},{6,4},{7,5},{4,6},{5,7},{10,8},{11,9},{8,1... | collective-permute-start | bytes 405512 | tf_op jit(solution)/shard_map/ppermute | solution.py:65
  23.0 0.7 collective-permute-start.16
  23.7 1.3 %collective-permute-start.4 = (bf16[528,128]{1,0:T(8,128)(2,1)S(1)}, bf16[528,128]{1,0:T(8,128)(2,1)S(1)}, u32[]{:S(2)}, u32[]{:S(2)}) collective-permute-start(bf16[528,128]{1,0:T(8,128)(2,1)S(1)} %collective-permute-done.1.refs_0_.refs_4_), channel_id=1, source_target_pairs={{3,0},{2,1},{1,2},{0,3},{7,4},{6,5},{5,6},{4,7},{11,8},{10,9},{9,1... | collective-permute-start | bytes 405512 | tf_op jit(solution)/shard_map/ppermute | solution.py:65
  25.0 1.5 %collective-permute-start.9 = (bf16[768,128]{1,0:T(8,128)(2,1)S(1)}, bf16[768,128]{1,0:T(8,128)(2,1)S(1)}, u32[]{:S(2)}, u32[]{:S(2)}) collective-permute-start(bf16[768,128]{1,0:T(8,128)(2,1)S(1)} %collective-permute-done.refs_0_.refs_12_), channel_id=1, source_target_pairs={{1,0},{0,1},{3,2},{2,3},{5,4},{4,5},{7,6},{6,7},{9,8},{8,9},{11,10... | collective-permute-start | bytes 589832 | tf_op jit(solution)/shard_map/ppermute | solution.py:65
  26.4 0.8 collective-permute-start.10
  27.2 0.6 collective-permute-start.5
  27.9 0.7 copy-done.2
  28.5 2.2 %collective-permute-done.4.refs_3_.refs_7_ = bf16[528,128]{1,0:T(8,128)(2,1)S(1)} collective-permute-done((bf16[528,128]{1,0:T(8,128)(2,1)S(1)}, bf16[528,128]{1,0:T(8,128)(2,1)S(1)}, u32[]{:S(2)}, u32[]{:S(2)}) %collective-permute-start.4) | collective-permute-done | bytes 135200 | tf_op jit(solution)/shard_map/ppermute | solution.py:65
  30.7 0.6 collective-permute-start.12
  31.4 4.9 %collective-permute-start.18 = (bf16[768,128]{1,0:T(8,128)(2,1)S(1)}, bf16[768,128]{1,0:T(8,128)(2,1)S(1)}, u32[]{:S(2)}, u32[]{:S(2)}) collective-permute-start(bf16[768,128]{1,0:T(8,128)(2,1)S(1)} %collective-permute-done.16.refs_8_.refs_20_), channel_id=1, source_target_pairs={{2,0},{3,1},{0,2},{1,3},{6,4},{7,5},{4,6},{5,7},{10,8},{11,9},{8,1... | collective-permute-start | bytes 589832 | tf_op jit(solution)/shard_map/ppermute | solution.py:65
  36.2 0.7 copy-done.14
  36.9 0.7 copy-done.5
  37.6 0.5 collective-permute-start.7
  38.1 0.7 copy-done.8
  38.7 0.7 copy-done.11
  39.4 1.8 %collective-permute-start.11 = (bf16[768,128]{1,0:T(8,128)(2,1)S(1)}, bf16[768,128]{1,0:T(8,128)(2,1)S(1)}, u32[]{:S(2)}, u32[]{:S(2)}) collective-permute-start(bf16[768,128]{1,0:T(8,128)(2,1)S(1)} %collective-permute-done.9.refs_1_.refs_13_), channel_id=1, source_target_pairs={{2,0},{3,1},{0,2},{1,3},{6,4},{7,5},{4,6},{5,7},{10,8},{11,9},{8,1... | collective-permute-start | bytes 589832 | tf_op jit(solution)/shard_map/ppermute | solution.py:65
  41.2 0.7 copy-done.17
  41.8 0.1 collective-permute-start.13
  41.9 0.6 copy-done.20
  42.5 0.6 collective-permute-start.17
  43.1 0.7 copy-done.23
  43.8 1.6 %collective-permute-start.19 = (bf16[768,128]{1,0:T(8,128)(2,1)S(1)}, bf16[768,128]{1,0:T(8,128)(2,1)S(1)}, u32[]{:S(2)}, u32[]{:S(2)}) collective-permute-start(bf16[768,128]{1,0:T(8,128)(2,1)S(1)} %collective-permute-done.18.refs_10_.refs_22_), channel_id=1, source_target_pairs={{1,0},{0,1},{3,2},{2,3},{5,4},{4,5},{7,6},{6,7},{9,8},{8,9},{11,10... | collective-permute-start | bytes 589832 | tf_op jit(solution)/shard_map/ppermute | solution.py:65
  45.4 1.3 %collective-permute-done.11.refs_3_.refs_15_ = bf16[768,128]{1,0:T(8,128)(2,1)S(1)} collective-permute-done((bf16[768,128]{1,0:T(8,128)(2,1)S(1)}, bf16[768,128]{1,0:T(8,128)(2,1)S(1)}, u32[]{:S(2)}, u32[]{:S(2)}) %collective-permute-start.11) | collective-permute-done | bytes 196640 | tf_op jit(solution)/shard_map/ppermute | solution.py:65
  46.7 0.5 collective-permute-start.22
  47.2 3.0 %collective-permute-done.17.refs_9_.refs_21_ = bf16[768,128]{1,0:T(8,128)(2,1)S(1)} collective-permute-done((bf16[768,128]{1,0:T(8,128)(2,1)S(1)}, bf16[768,128]{1,0:T(8,128)(2,1)S(1)}, u32[]{:S(2)}, u32[]{:S(2)}) %collective-permute-start.17) | collective-permute-done | bytes 196640 | tf_op jit(solution)/shard_map/ppermute | solution.py:65
  50.3 0.5 collective-permute-start.21
  50.8 3.2 %collective-permute-done.19.refs_11_.refs_23_ = bf16[768,128]{1,0:T(8,128)(2,1)S(1)} collective-permute-done((bf16[768,128]{1,0:T(8,128)(2,1)S(1)}, bf16[768,128]{1,0:T(8,128)(2,1)S(1)}, u32[]{:S(2)}, u32[]{:S(2)}) %collective-permute-start.19) | collective-permute-done | bytes 196640 | tf_op jit(solution)/shard_map/ppermute | solution.py:65
  54.0 0.1 pad_add_fusion.place_ref
  54.1 0.9 copy-done.3
  55.0 0.9 copy-done.6
  55.9 0.9 copy-done.9
  56.8 0.9 copy-done.12
  57.7 0.9 copy-done.15
  58.6 0.9 copy-done.18
  59.5 0.9 copy-done.21
  60.4 0.9 copy-done.24
  61.3 0.9 copy-done.26
  62.3 1.3 %shard_map.102 = (bf16[144,128]{1,0:T(8,128)(2,1)S(1)}, bf16[144,128]{1,0:T(8,128)(2,1)S(1)}, bf16[144,128]{1,0:T(8,128)(2,1)S(1)}, bf16[144,128]{1,0:T(8,128)(2,1)S(1)}) custom-call(s32[3]{0:T(128)S(1)} %pad_add_fusion.place_ref, bf16[128,1024]{1,0:T(8,128)(2,1)S(1)} %bitcast.21, bf16[128,1024]{1,0:T(8,128)(2,1)S(1)} %bitcast.23, ...), custom_call_target="tpu_custom_call" | custom-call | tf_op jit(solution)/shard_map/pallas_call | solution.py:375
  63.6 1.4 %shard_map.103 = (bf16[128,384]{1,0:T(8,128)(2,1)S(1)}, bf16[128,384]{1,0:T(8,128)(2,1)S(1)}, bf16[128,384]{1,0:T(8,128)(2,1)S(1)}, bf16[128,384]{1,0:T(8,128)(2,1)S(1)}) custom-call(s32[3]{0:T(128)S(1)} %pad_add_fusion.place_ref, bf16[128,1024]{1,0:T(8,128)(2,1)S(1)} %bitcast.22, bf16[768,128]{1,0:T(8,128)(2,1)S(1)} %collective-permute-done.refs_0_.refs_12_, ...), custom_call_target="tpu_custom_call" | custom-call | tf_op jit(solution)/shard_map/pallas_call | solution.py:375
  65.0 0.1 collective-permute-start.24
  65.1 0.7 collective-permute-start.25
  65.8 3.6 %collective-permute-start.26 = (bf16[128,384]{1,0:T(8,128)(2,1)S(1)}, bf16[128,384]{1,0:T(8,128)(2,1)S(1)}, u32[]{:S(2)}, u32[]{:S(2)}) collective-permute-start(bf16[128,384]{1,0:T(8,128)(2,1)S(1)} %get-tuple-element.35), channel_id=1, source_target_pairs={{0,12},{4,8},{8,4},{12,0},{1,13},{5,9},{9,5},{13,1},{2,14},{6,10},... | collective-permute-start | bytes 294920 | tf_op jit(solution)/shard_map/ppermute | solution.py:76
  69.5 0.7 collective-permute-start.29
  70.2 1.2 %collective-permute-done.24 = bf16[128,384]{1,0:T(8,128)(2,1)S(1)} collective-permute-done((bf16[128,384]{1,0:T(8,128)(2,1)S(1)}, bf16[128,384]{1,0:T(8,128)(2,1)S(1)}, u32[]{:S(2)}, u32[]{:S(2)}) %collective-permute-start.24) | collective-permute-done | bytes 98336 | tf_op jit(solution)/shard_map/ppermute | solution.py:76
  71.4 2.4 %collective-permute-start.30 = (bf16[144,128]{1,0:T(8,128)(2,1)S(1)}, bf16[144,128]{1,0:T(8,128)(2,1)S(1)}, u32[]{:S(2)}, u32[]{:S(2)}) collective-permute-start(bf16[144,128]{1,0:T(8,128)(2,1)S(1)} %get-tuple-element.38), channel_id=1, source_target_pairs={{0,12},{4,8},{8,4},{12,0},{1,13},{5,9},{9,5},{13,1},{2,14},{6,10},... | collective-permute-start | bytes 110600 | tf_op jit(solution)/shard_map/ppermute | solution.py:76
  73.9 3.7 %collective-permute-done.25 = bf16[128,384]{1,0:T(8,128)(2,1)S(1)} collective-permute-done((bf16[128,384]{1,0:T(8,128)(2,1)S(1)}, bf16[128,384]{1,0:T(8,128)(2,1)S(1)}, u32[]{:S(2)}, u32[]{:S(2)}) %collective-permute-start.25) | collective-permute-done | bytes 98336 | tf_op jit(solution)/shard_map/ppermute | solution.py:76
  77.6 0.1 collective-permute-start.27
  77.7 2.7 %collective-permute-done.29 = bf16[144,128]{1,0:T(8,128)(2,1)S(1)} collective-permute-done((bf16[144,128]{1,0:T(8,128)(2,1)S(1)}, bf16[144,128]{1,0:T(8,128)(2,1)S(1)}, u32[]{:S(2)}, u32[]{:S(2)}) %collective-permute-start.29) | collective-permute-done | bytes 36896 | tf_op jit(solution)/shard_map/ppermute | solution.py:76
  80.5 1.3 %collective-permute-done.31.refs_3_ = f32[144,128]{1,0:T(8,128)S(1)} collective-permute-done((f32[144,128]{1,0:T(8,128)S(1)}, f32[144,128]{1,0:T(8,128)S(1)}, u32[]{:S(2)}, u32[]{:S(2)}) %collective-permute-start.31) | collective-permute-done | bytes 73760 | tf_op jit(solution)/shard_map/ppermute | solution.py:65
  81.9 10.8 %shard_map.104 = (bf16[144,512]{1,0:T(8,128)(2,1)S(1)}, f32[64,256]{1,0:T(8,128)S(1)}, f32[64,256]{1,0:T(8,128)S(1)}, f32[64,256]{1,0:T(8,128)S(1)}, f32[64,256]{1,0:T(8,128)S(1)}) custom-call(s32[3]{0:T(128)S(1)} %pad_add_fusion.place_ref, f32[128,384]{1,0:T(8,128)S(1)} %convert_add_fusion.refs_0_, f32[128,384]{1,0:T(8,128)S(1)} %collective-permute-done.27.refs_1_, ...), custom_call_target="tpu_custom_call" | custom-call | tf_op jit(solution)/shard_map/pallas_call | solution.py:375
  92.7 1.0 collective-permute-start.32
  93.8 0.9 collective-permute-start.33
  94.7 2.5 %collective-permute-start.34 = (bf16[144,512]{1,0:T(8,128)(2,1)S(1)}, bf16[144,512]{1,0:T(8,128)(2,1)S(1)}, u32[]{:S(2)}, u32[]{:S(2)}) collective-permute-start(bf16[144,512]{1,0:T(8,128)(2,1)S(1)} %get-tuple-element.39.refs_0_), channel_id=1, source_target_pairs={{12,0},{8,4},{4,8},{0,12},{13,1},{9,5},{5,9},{1,13},{14,2},{10,6},... | collective-permute-start | bytes 442376 | tf_op jit(solution)/shard_map/ppermute | solution.py:65
  97.2 3.4 %collective-permute-done.32.refs_1_ = bf16[144,512]{1,0:T(8,128)(2,1)S(1)} collective-permute-done((bf16[144,512]{1,0:T(8,128)(2,1)S(1)}, bf16[144,512]{1,0:T(8,128)(2,1)S(1)}, u32[]{:S(2)}, u32[]{:S(2)}) %collective-permute-start.32) | collective-permute-done | bytes 147488 | tf_op jit(solution)/shard_map/ppermute | solution.py:65
  100.6 0.5 collective-permute-start.35
  101.0 0.7 collective-permute-start.36
  101.8 2.3 %collective-permute-start.37 = (f32[64,256]{1,0:T(8,128)S(1)}, f32[64,256]{1,0:T(8,128)S(1)}, u32[]{:S(2)}, u32[]{:S(2)}) collective-permute-start(f32[64,256]{1,0:T(8,128)S(1)} %get-tuple-element.49), channel_id=1, source_target_pairs={{0,3},{1,2},{2,1},{3,0},{4,7},{5,6},{6,5},{7,4},{8,11},{9,10},{10,... | collective-permute-start | bytes 196616 | tf_op jit(solution)/shard_map/ppermute | solution.py:76
  104.1 3.6 %collective-permute-done.33.refs_2_ = bf16[144,512]{1,0:T(8,128)(2,1)S(1)} collective-permute-done((bf16[144,512]{1,0:T(8,128)(2,1)S(1)}, bf16[144,512]{1,0:T(8,128)(2,1)S(1)}, u32[]{:S(2)}, u32[]{:S(2)}) %collective-permute-start.33) | collective-permute-done | bytes 147488 | tf_op jit(solution)/shard_map/ppermute | solution.py:65
  107.7 3.2 %shard_map.105 = (bf16[128,1024]{1,0:T(8,128)(2,1)}, bf16[128,1024]{1,0:T(8,128)(2,1)}) custom-call(s32[3]{0:T(128)S(1)} %pad_add_fusion.place_ref, bf16[144,512]{1,0:T(8,128)(2,1)S(1)} %get-tuple-element.39.refs_0_, bf16[144,512]{1,0:T(8,128)(2,1)S(1)} %collective-permute-done.32.refs_1_, bf16[144,512]{1,0:T(8,128)(2,1)S(1)} %collective-permute-done.33.refs_2_, ...), custom_call_target="tpu_custom_call" | custom-call | tf_op jit(solution)/shard_map/pallas_call | solution.py:375
  111.0 0.6 slice_bitcast_fusion
  (85 shorter events, 0.5 us)
Async XLA Ops:
  0.6 2.0 %copy-start = (bf16[4096,1]{0,1:T(2,128)(2,1)S(1)}, bf16[4096,1]{0,1:T(2,128)(2,1)}, u32[]{:S(2)}) copy-start(bf16[4096,1]{0,1:T(2,128)(2,1)} %param.9) | copy-start | bytes 24580
  0.6 2.0 %copy-start.29 = (bf16[512,128]{1,0:T(8,128)(2,1)S(1)}, bf16[512,128]{1,0:T(8,128)(2,1)}, u32[]{:S(2)}) copy-start(bf16[512,128]{1,0:T(8,128)(2,1)} %param.10) | copy-start | bytes 393220
  1.7 52.3 %copy-start.1 = (bf16[1,128,1024]{2,1,0:T(8,128)(2,1)S(1)}, bf16[1,128,1024]{2,1,0:T(8,128)(2,1)}, u32[]{:S(2)}) copy-start(bf16[1,128,1024]{2,1,0:T(8,128)(2,1)} %param.7) | copy-start | bytes 786436
  1.8 1.6 %collective-permute-start = (bf16[768,128]{1,0:T(8,128)(2,1)S(1)}, bf16[768,128]{1,0:T(8,128)(2,1)S(1)}, u32[]{:S(2)}, u32[]{:S(2)}) collective-permute-start(bf16[768,128]{1,0:T(8,128)(2,1)S(1)} %bitcast.28), channel_id=1, source_target_pairs={{0,0},{1,1},{2,4},{3,5},{4,2},{5,3},{6,6},{7,7},{8,16},{9,17},{10,... | collective-permute-start | bytes 589832 | tf_op jit(solution)/shard_map/ppermute | solution.py:405
  2.7 0.7 collective-permute-start.1
  3.4 23.1 %collective-permute-start.2 = (bf16[528,128]{1,0:T(8,128)(2,1)S(1)}, bf16[528,128]{1,0:T(8,128)(2,1)S(1)}, u32[]{:S(2)}, u32[]{:S(2)}) collective-permute-start(bf16[528,128]{1,0:T(8,128)(2,1)S(1)} %collective-permute-done.1.refs_0_.refs_4_), channel_id=1, source_target_pairs={{1,0},{0,1},{3,2},{2,3},{5,4},{4,5},{7,6},{6,7},{9,8},{8,9},{11,10... | collective-permute-start | bytes 405512 | tf_op jit(solution)/shard_map/ppermute | solution.py:65
  6.4 20.8 %collective-permute-start.3 = (bf16[528,128]{1,0:T(8,128)(2,1)S(1)}, bf16[528,128]{1,0:T(8,128)(2,1)S(1)}, u32[]{:S(2)}, u32[]{:S(2)}) collective-permute-start(bf16[528,128]{1,0:T(8,128)(2,1)S(1)} %collective-permute-done.1.refs_0_.refs_4_), channel_id=1, source_target_pairs={{2,0},{3,1},{0,2},{1,3},{6,4},{7,5},{4,6},{5,7},{10,8},{11,9},{8,1... | collective-permute-start | bytes 405512 | tf_op jit(solution)/shard_map/ppermute | solution.py:65
  23.0 8.4 %collective-permute-start.16 = (bf16[768,128]{1,0:T(8,128)(2,1)S(1)}, bf16[768,128]{1,0:T(8,128)(2,1)S(1)}, u32[]{:S(2)}, u32[]{:S(2)}) collective-permute-start(bf16[768,128]{1,0:T(8,128)(2,1)S(1)} %bitcast.27), channel_id=1, source_target_pairs={{0,0},{1,1},{2,4},{3,5},{4,2},{5,3},{6,6},{7,7},{8,16},{9,17},{10,... | collective-permute-start | bytes 589832 | tf_op jit(solution)/shard_map/ppermute | solution.py:405
  23.7 7.0 %collective-permute-start.4 = (bf16[528,128]{1,0:T(8,128)(2,1)S(1)}, bf16[528,128]{1,0:T(8,128)(2,1)S(1)}, u32[]{:S(2)}, u32[]{:S(2)}) collective-permute-start(bf16[528,128]{1,0:T(8,128)(2,1)S(1)} %collective-permute-done.1.refs_0_.refs_4_), channel_id=1, source_target_pairs={{3,0},{2,1},{1,2},{0,3},{7,4},{6,5},{5,6},{4,7},{11,8},{10,9},{9,1... | collective-permute-start | bytes 405512 | tf_op jit(solution)/shard_map/ppermute | solution.py:65
  25.0 12.6 %collective-permute-start.9 = (bf16[768,128]{1,0:T(8,128)(2,1)S(1)}, bf16[768,128]{1,0:T(8,128)(2,1)S(1)}, u32[]{:S(2)}, u32[]{:S(2)}) collective-permute-start(bf16[768,128]{1,0:T(8,128)(2,1)S(1)} %collective-permute-done.refs_0_.refs_12_), channel_id=1, source_target_pairs={{1,0},{0,1},{3,2},{2,3},{5,4},{4,5},{7,6},{6,7},{9,8},{8,9},{11,10... | collective-permute-start | bytes 589832 | tf_op jit(solution)/shard_map/ppermute | solution.py:65
  26.4 12.3 %collective-permute-start.10 = (bf16[768,128]{1,0:T(8,128)(2,1)S(1)}, bf16[768,128]{1,0:T(8,128)(2,1)S(1)}, u32[]{:S(2)}, u32[]{:S(2)}) collective-permute-start(bf16[768,128]{1,0:T(8,128)(2,1)S(1)} %collective-permute-done.refs_0_.refs_12_), channel_id=1, source_target_pairs={{2,0},{3,1},{0,2},{1,3},{6,4},{7,5},{4,6},{5,7},{10,8},{11,9},{8,1... | collective-permute-start | bytes 589832 | tf_op jit(solution)/shard_map/ppermute | solution.py:65
  27.2 9.0 %collective-permute-start.5 = (bf16[528,128]{1,0:T(8,128)(2,1)S(1)}, bf16[528,128]{1,0:T(8,128)(2,1)S(1)}, u32[]{:S(2)}, u32[]{:S(2)}) collective-permute-start(bf16[528,128]{1,0:T(8,128)(2,1)S(1)} %collective-permute-done.1.refs_0_.refs_4_), channel_id=1, source_target_pairs={{16,0},{0,16},{17,1},{1,17},{18,2},{2,18},{19,3},{3,19},{20,4},{4,... | collective-permute-start | bytes 405512 | tf_op jit(solution)/shard_map/ppermute | solution.py:65
  30.7 8.7 %collective-permute-start.12 = (bf16[768,128]{1,0:T(8,128)(2,1)S(1)}, bf16[768,128]{1,0:T(8,128)(2,1)S(1)}, u32[]{:S(2)}, u32[]{:S(2)}) collective-permute-start(bf16[768,128]{1,0:T(8,128)(2,1)S(1)} %collective-permute-done.refs_0_.refs_12_), channel_id=1, source_target_pairs={{16,0},{0,16},{17,1},{1,17},{18,2},{2,18},{19,3},{3,19},{20,4},{4,... | collective-permute-start | bytes 589832 | tf_op jit(solution)/shard_map/ppermute | solution.py:65
  31.4 12.5 %collective-permute-start.18 = (bf16[768,128]{1,0:T(8,128)(2,1)S(1)}, bf16[768,128]{1,0:T(8,128)(2,1)S(1)}, u32[]{:S(2)}, u32[]{:S(2)}) collective-permute-start(bf16[768,128]{1,0:T(8,128)(2,1)S(1)} %collective-permute-done.16.refs_8_.refs_20_), channel_id=1, source_target_pairs={{2,0},{3,1},{0,2},{1,3},{6,4},{7,5},{4,6},{5,7},{10,8},{11,9},{8,1... | collective-permute-start | bytes 589832 | tf_op jit(solution)/shard_map/ppermute | solution.py:65
  36.9 4.3 %collective-permute-start.6 = (bf16[528,128]{1,0:T(8,128)(2,1)S(1)}, bf16[528,128]{1,0:T(8,128)(2,1)S(1)}, u32[]{:S(2)}, u32[]{:S(2)}) collective-permute-start(bf16[528,128]{1,0:T(8,128)(2,1)S(1)} %collective-permute-done.2.refs_1_.refs_5_), channel_id=1, source_target_pairs={{16,0},{0,16},{17,1},{1,17},{18,2},{2,18},{19,3},{3,19},{20,4},{4,... | collective-permute-start | bytes 405512 | tf_op jit(solution)/shard_map/ppermute | solution.py:65
  36.9 0.7 copy-start.5
  37.6 4.3 %collective-permute-start.7 = (bf16[528,128]{1,0:T(8,128)(2,1)S(1)}, bf16[528,128]{1,0:T(8,128)(2,1)S(1)}, u32[]{:S(2)}, u32[]{:S(2)}) collective-permute-start(bf16[528,128]{1,0:T(8,128)(2,1)S(1)} %collective-permute-done.3.refs_2_.refs_6_), channel_id=1, source_target_pairs={{16,0},{0,16},{17,1},{1,17},{18,2},{2,18},{19,3},{3,19},{20,4},{4,... | collective-permute-start | bytes 405512 | tf_op jit(solution)/shard_map/ppermute | solution.py:65
  38.7 4.4 %collective-permute-start.8 = (bf16[528,128]{1,0:T(8,128)(2,1)S(1)}, bf16[528,128]{1,0:T(8,128)(2,1)S(1)}, u32[]{:S(2)}, u32[]{:S(2)}) collective-permute-start(bf16[528,128]{1,0:T(8,128)(2,1)S(1)} %collective-permute-done.4.refs_3_.refs_7_), channel_id=1, source_target_pairs={{16,0},{0,16},{17,1},{1,17},{18,2},{2,18},{19,3},{3,19},{20,4},{4,... | collective-permute-start | bytes 405512 | tf_op jit(solution)/shard_map/ppermute | solution.py:65
  38.7 0.7 copy-start.11
  39.4 7.3 %collective-permute-start.11 = (bf16[768,128]{1,0:T(8,128)(2,1)S(1)}, bf16[768,128]{1,0:T(8,128)(2,1)S(1)}, u32[]{:S(2)}, u32[]{:S(2)}) collective-permute-start(bf16[768,128]{1,0:T(8,128)(2,1)S(1)} %collective-permute-done.9.refs_1_.refs_13_), channel_id=1, source_target_pairs={{2,0},{3,1},{0,2},{1,3},{6,4},{7,5},{4,6},{5,7},{10,8},{11,9},{8,1... | collective-permute-start | bytes 589832 | tf_op jit(solution)/shard_map/ppermute | solution.py:65
  41.1 0.7 copy-start.17
  41.8 4.9 %collective-permute-start.13 = (bf16[768,128]{1,0:T(8,128)(2,1)S(1)}, bf16[768,128]{1,0:T(8,128)(2,1)S(1)}, u32[]{:S(2)}, u32[]{:S(2)}) collective-permute-start(bf16[768,128]{1,0:T(8,128)(2,1)S(1)} %collective-permute-done.9.refs_1_.refs_13_), channel_id=1, source_target_pairs={{16,0},{0,16},{17,1},{1,17},{18,2},{2,18},{19,3},{3,19},{20,4},{4,... | collective-permute-start | bytes 589832 | tf_op jit(solution)/shard_map/ppermute | solution.py:65
  42.5 7.7 %collective-permute-start.17 = (bf16[768,128]{1,0:T(8,128)(2,1)S(1)}, bf16[768,128]{1,0:T(8,128)(2,1)S(1)}, u32[]{:S(2)}, u32[]{:S(2)}) collective-permute-start(bf16[768,128]{1,0:T(8,128)(2,1)S(1)} %collective-permute-done.16.refs_8_.refs_20_), channel_id=1, source_target_pairs={{1,0},{0,1},{3,2},{2,3},{5,4},{4,5},{7,6},{6,7},{9,8},{8,9},{11,10... | collective-permute-start | bytes 589832 | tf_op jit(solution)/shard_map/ppermute | solution.py:65
  43.1 0.7 copy-start.23
  43.8 6.5 %collective-permute-start.14 = (bf16[768,128]{1,0:T(8,128)(2,1)S(1)}, bf16[768,128]{1,0:T(8,128)(2,1)S(1)}, u32[]{:S(2)}, u32[]{:S(2)}) collective-permute-start(bf16[768,128]{1,0:T(8,128)(2,1)S(1)} %collective-permute-done.10.refs_2_.refs_14_), channel_id=1, source_target_pairs={{16,0},{0,16},{17,1},{1,17},{18,2},{2,18},{19,3},{3,19},{20,4},{4,... | collective-permute-start | bytes 589832 | tf_op jit(solution)/shard_map/ppermute | solution.py:65
  43.8 10.2 %collective-permute-start.19 = (bf16[768,128]{1,0:T(8,128)(2,1)S(1)}, bf16[768,128]{1,0:T(8,128)(2,1)S(1)}, u32[]{:S(2)}, u32[]{:S(2)}) collective-permute-start(bf16[768,128]{1,0:T(8,128)(2,1)S(1)} %collective-permute-done.18.refs_10_.refs_22_), channel_id=1, source_target_pairs={{1,0},{0,1},{3,2},{2,3},{5,4},{4,5},{7,6},{6,7},{9,8},{8,9},{11,10... | collective-permute-start | bytes 589832 | tf_op jit(solution)/shard_map/ppermute | solution.py:65
  46.7 16.9 %collective-permute-start.20 = (bf16[768,128]{1,0:T(8,128)(2,1)S(1)}, bf16[768,128]{1,0:T(8,128)(2,1)S(1)}, u32[]{:S(2)}, u32[]{:S(2)}) collective-permute-start(bf16[768,128]{1,0:T(8,128)(2,1)S(1)} %collective-permute-done.16.refs_8_.refs_20_), channel_id=1, source_target_pairs={{16,0},{0,16},{17,1},{1,17},{18,2},{2,18},{19,3},{3,19},{20,4},{4,... | collective-permute-start | bytes 589832 | tf_op jit(solution)/shard_map/ppermute | solution.py:65
  46.7 16.9 %collective-permute-start.22 = (bf16[768,128]{1,0:T(8,128)(2,1)S(1)}, bf16[768,128]{1,0:T(8,128)(2,1)S(1)}, u32[]{:S(2)}, u32[]{:S(2)}) collective-permute-start(bf16[768,128]{1,0:T(8,128)(2,1)S(1)} %collective-permute-done.18.refs_10_.refs_22_), channel_id=1, source_target_pairs={{16,0},{0,16},{17,1},{1,17},{18,2},{2,18},{19,3},{3,19},{20,4},{4,... | collective-permute-start | bytes 589832 | tf_op jit(solution)/shard_map/ppermute | solution.py:65
  50.3 13.3 %collective-permute-start.15 = (bf16[768,128]{1,0:T(8,128)(2,1)S(1)}, bf16[768,128]{1,0:T(8,128)(2,1)S(1)}, u32[]{:S(2)}, u32[]{:S(2)}) collective-permute-start(bf16[768,128]{1,0:T(8,128)(2,1)S(1)} %collective-permute-done.11.refs_3_.refs_15_), channel_id=1, source_target_pairs={{16,0},{0,16},{17,1},{1,17},{18,2},{2,18},{19,3},{3,19},{20,4},{4,... | collective-permute-start | bytes 589832 | tf_op jit(solution)/shard_map/ppermute | solution.py:65
  50.3 13.4 %collective-permute-start.21 = (bf16[768,128]{1,0:T(8,128)(2,1)S(1)}, bf16[768,128]{1,0:T(8,128)(2,1)S(1)}, u32[]{:S(2)}, u32[]{:S(2)}) collective-permute-start(bf16[768,128]{1,0:T(8,128)(2,1)S(1)} %collective-permute-done.17.refs_9_.refs_21_), channel_id=1, source_target_pairs={{16,0},{0,16},{17,1},{1,17},{18,2},{2,18},{19,3},{3,19},{20,4},{4,... | collective-permute-start | bytes 589832 | tf_op jit(solution)/shard_map/ppermute | solution.py:65
  54.0 9.6 %collective-permute-start.23 = (bf16[768,128]{1,0:T(8,128)(2,1)S(1)}, bf16[768,128]{1,0:T(8,128)(2,1)S(1)}, u32[]{:S(2)}, u32[]{:S(2)}) collective-permute-start(bf16[768,128]{1,0:T(8,128)(2,1)S(1)} %collective-permute-done.19.refs_11_.refs_23_), channel_id=1, source_target_pairs={{16,0},{0,16},{17,1},{1,17},{18,2},{2,18},{19,3},{3,19},{20,4},{4,... | collective-permute-start | bytes 589832 | tf_op jit(solution)/shard_map/ppermute | solution.py:65
  54.1 0.9 copy-start.3
  55.0 0.9 copy-start.6
  55.9 0.9 copy-start.9
  56.8 0.9 copy-start.12
  57.7 0.9 copy-start.15
  58.6 0.9 copy-start.18
  59.5 0.9 copy-start.21
  60.4 0.9 copy-start.24
  61.3 0.9 copy-start.26
  65.0 6.4 %collective-permute-start.24 = (bf16[128,384]{1,0:T(8,128)(2,1)S(1)}, bf16[128,384]{1,0:T(8,128)(2,1)S(1)}, u32[]{:S(2)}, u32[]{:S(2)}) collective-permute-start(bf16[128,384]{1,0:T(8,128)(2,1)S(1)} %get-tuple-element.33), channel_id=1, source_target_pairs={{0,4},{4,0},{8,12},{12,8},{1,5},{5,1},{9,13},{13,9},{2,6},{6,2},{1... | collective-permute-start | bytes 294920 | tf_op jit(solution)/shard_map/ppermute | solution.py:76
  65.1 12.4 %collective-permute-start.25 = (bf16[128,384]{1,0:T(8,128)(2,1)S(1)}, bf16[128,384]{1,0:T(8,128)(2,1)S(1)}, u32[]{:S(2)}, u32[]{:S(2)}) collective-permute-start(bf16[128,384]{1,0:T(8,128)(2,1)S(1)} %get-tuple-element.34), channel_id=1, source_target_pairs={{0,8},{4,12},{8,0},{12,4},{1,9},{5,13},{9,1},{13,5},{2,10},{6,14},... | collective-permute-start | bytes 294920 | tf_op jit(solution)/shard_map/ppermute | solution.py:76
  65.8 11.7 %collective-permute-start.26 = (bf16[128,384]{1,0:T(8,128)(2,1)S(1)}, bf16[128,384]{1,0:T(8,128)(2,1)S(1)}, u32[]{:S(2)}, u32[]{:S(2)}) collective-permute-start(bf16[128,384]{1,0:T(8,128)(2,1)S(1)} %get-tuple-element.35), channel_id=1, source_target_pairs={{0,12},{4,8},{8,4},{12,0},{1,13},{5,9},{9,5},{13,1},{2,14},{6,10},... | collective-permute-start | bytes 294920 | tf_op jit(solution)/shard_map/ppermute | solution.py:76
  69.5 8.2 %collective-permute-start.28 = (bf16[144,128]{1,0:T(8,128)(2,1)S(1)}, bf16[144,128]{1,0:T(8,128)(2,1)S(1)}, u32[]{:S(2)}, u32[]{:S(2)}) collective-permute-start(bf16[144,128]{1,0:T(8,128)(2,1)S(1)} %get-tuple-element.36), channel_id=1, source_target_pairs={{0,4},{4,0},{8,12},{12,8},{1,5},{5,1},{9,13},{13,9},{2,6},{6,2},{1... | collective-permute-start | bytes 110600 | tf_op jit(solution)/shard_map/ppermute | solution.py:76
  69.5 11.0 %collective-permute-start.29 = (bf16[144,128]{1,0:T(8,128)(2,1)S(1)}, bf16[144,128]{1,0:T(8,128)(2,1)S(1)}, u32[]{:S(2)}, u32[]{:S(2)}) collective-permute-start(bf16[144,128]{1,0:T(8,128)(2,1)S(1)} %get-tuple-element.37), channel_id=1, source_target_pairs={{0,8},{4,12},{8,0},{12,4},{1,9},{5,13},{9,1},{13,5},{2,10},{6,14},... | collective-permute-start | bytes 110600 | tf_op jit(solution)/shard_map/ppermute | solution.py:76
  71.4 9.0 %collective-permute-start.30 = (bf16[144,128]{1,0:T(8,128)(2,1)S(1)}, bf16[144,128]{1,0:T(8,128)(2,1)S(1)}, u32[]{:S(2)}, u32[]{:S(2)}) collective-permute-start(bf16[144,128]{1,0:T(8,128)(2,1)S(1)} %get-tuple-element.38), channel_id=1, source_target_pairs={{0,12},{4,8},{8,4},{12,0},{1,13},{5,9},{9,5},{13,1},{2,14},{6,10},... | collective-permute-start | bytes 110600 | tf_op jit(solution)/shard_map/ppermute | solution.py:76
  77.5 4.3 %copy-start.27 = (f32[1,128,512]{2,1,0:T(8,128)S(1)}, f32[1,128,512]{2,1,0:T(8,128)}, u32[]{:S(2)}) copy-start(f32[1,128,512]{2,1,0:T(8,128)} %param.11) | copy-start | bytes 786436
  77.5 4.3 %copy-start.28 = (f32[1,512,128]{2,1,0:T(8,128)S(1)}, f32[1,512,128]{2,1,0:T(8,128)}, u32[]{:S(2)}) copy-start(f32[1,512,128]{2,1,0:T(8,128)} %param.12) | copy-start | bytes 786436
  77.6 4.2 %collective-permute-start.27 = (f32[128,384]{1,0:T(8,128)S(1)}, f32[128,384]{1,0:T(8,128)S(1)}, u32[]{:S(2)}, u32[]{:S(2)}) collective-permute-start(f32[128,384]{1,0:T(8,128)S(1)} %convert_add_fusion.refs_0_), channel_id=1, source_target_pairs={{16,0},{0,16},{17,1},{1,17},{18,2},{2,18},{19,3},{3,19},{20,4},{4,... | collective-permute-start | bytes 589832 | tf_op jit(solution)/shard_map/ppermute | solution.py:65
  80.4 27.2 %copy-start.25 = (bf16[528,128]{1,0:T(8,128)(2,1)S(1)}, bf16[528,128]{1,0:T(8,128)(2,1)}, u32[]{:S(2)}) copy-start(bf16[528,128]{1,0:T(8,128)(2,1)} %copy-done.23) | copy-start | bytes 405508
  80.5 1.3 %collective-permute-start.31 = (f32[144,128]{1,0:T(8,128)S(1)}, f32[144,128]{1,0:T(8,128)S(1)}, u32[]{:S(2)}, u32[]{:S(2)}) collective-permute-start(f32[144,128]{1,0:T(8,128)S(1)} %convert_add_fusion.1.refs_2_), channel_id=1, source_target_pairs={{16,0},{0,16},{17,1},{1,17},{18,2},{2,18},{19,3},{3,19},{20,4},{4,... | collective-permute-start | bytes 221192 | tf_op jit(solution)/shard_map/ppermute | solution.py:65
  81.8 25.9 %copy-start.4 = (bf16[528,128]{1,0:T(8,128)(2,1)S(1)}, bf16[528,128]{1,0:T(8,128)(2,1)}, u32[]{:S(2)}) copy-start(bf16[528,128]{1,0:T(8,128)(2,1)} %copy-done.2) | copy-start | bytes 405508
  81.8 25.9 %copy-start.7 = (bf16[528,128]{1,0:T(8,128)(2,1)S(1)}, bf16[528,128]{1,0:T(8,128)(2,1)}, u32[]{:S(2)}) copy-start(bf16[528,128]{1,0:T(8,128)(2,1)} %copy-done.5) | copy-start | bytes 405508
  81.8 25.9 %copy-start.10 = (bf16[528,128]{1,0:T(8,128)(2,1)S(1)}, bf16[528,128]{1,0:T(8,128)(2,1)}, u32[]{:S(2)}) copy-start(bf16[528,128]{1,0:T(8,128)(2,1)} %copy-done.8) | copy-start | bytes 405508
  81.8 25.9 %copy-start.13 = (bf16[528,128]{1,0:T(8,128)(2,1)S(1)}, bf16[528,128]{1,0:T(8,128)(2,1)}, u32[]{:S(2)}) copy-start(bf16[528,128]{1,0:T(8,128)(2,1)} %copy-done.11) | copy-start | bytes 405508
  81.9 25.9 %copy-start.16 = (bf16[528,128]{1,0:T(8,128)(2,1)S(1)}, bf16[528,128]{1,0:T(8,128)(2,1)}, u32[]{:S(2)}) copy-start(bf16[528,128]{1,0:T(8,128)(2,1)} %copy-done.14) | copy-start | bytes 405508
  81.9 25.9 %copy-start.19 = (bf16[528,128]{1,0:T(8,128)(2,1)S(1)}, bf16[528,128]{1,0:T(8,128)(2,1)}, u32[]{:S(2)}) copy-start(bf16[528,128]{1,0:T(8,128)(2,1)} %copy-done.17) | copy-start | bytes 405508
  81.9 25.9 %copy-start.22 = (bf16[528,128]{1,0:T(8,128)(2,1)S(1)}, bf16[528,128]{1,0:T(8,128)(2,1)}, u32[]{:S(2)}) copy-start(bf16[528,128]{1,0:T(8,128)(2,1)} %copy-done.20) | copy-start | bytes 405508
  92.7 7.8 %collective-permute-start.32 = (bf16[144,512]{1,0:T(8,128)(2,1)S(1)}, bf16[144,512]{1,0:T(8,128)(2,1)S(1)}, u32[]{:S(2)}, u32[]{:S(2)}) collective-permute-start(bf16[144,512]{1,0:T(8,128)(2,1)S(1)} %get-tuple-element.39.refs_0_), channel_id=1, source_target_pairs={{4,0},{0,4},{12,8},{8,12},{5,1},{1,5},{13,9},{9,13},{6,2},{2,6},{1... | collective-permute-start | bytes 442376 | tf_op jit(solution)/shard_map/ppermute | solution.py:65
  93.8 13.9 %collective-permute-start.33 = (bf16[144,512]{1,0:T(8,128)(2,1)S(1)}, bf16[144,512]{1,0:T(8,128)(2,1)S(1)}, u32[]{:S(2)}, u32[]{:S(2)}) collective-permute-start(bf16[144,512]{1,0:T(8,128)(2,1)S(1)} %get-tuple-element.39.refs_0_), channel_id=1, source_target_pairs={{8,0},{12,4},{0,8},{4,12},{9,1},{13,5},{1,9},{5,13},{10,2},{14,6},... | collective-permute-start | bytes 442376 | tf_op jit(solution)/shard_map/ppermute | solution.py:65
  94.7 13.0 %collective-permute-start.34 = (bf16[144,512]{1,0:T(8,128)(2,1)S(1)}, bf16[144,512]{1,0:T(8,128)(2,1)S(1)}, u32[]{:S(2)}, u32[]{:S(2)}) collective-permute-start(bf16[144,512]{1,0:T(8,128)(2,1)S(1)} %get-tuple-element.39.refs_0_), channel_id=1, source_target_pairs={{12,0},{8,4},{4,8},{0,12},{13,1},{9,5},{5,9},{1,13},{14,2},{10,6},... | collective-permute-start | bytes 442376 | tf_op jit(solution)/shard_map/ppermute | solution.py:65
  100.6 10.3 %collective-permute-start.35 = (f32[64,256]{1,0:T(8,128)S(1)}, f32[64,256]{1,0:T(8,128)S(1)}, u32[]{:S(2)}, u32[]{:S(2)}) collective-permute-start(f32[64,256]{1,0:T(8,128)S(1)} %get-tuple-element.47), channel_id=1, source_target_pairs={{0,1},{1,0},{2,3},{3,2},{4,5},{5,4},{6,7},{7,6},{8,9},{9,8},{10,11... | collective-permute-start | bytes 196616 | tf_op jit(solution)/shard_map/ppermute | solution.py:76
  101.0 9.9 %collective-permute-start.36 = (f32[64,256]{1,0:T(8,128)S(1)}, f32[64,256]{1,0:T(8,128)S(1)}, u32[]{:S(2)}, u32[]{:S(2)}) collective-permute-start(f32[64,256]{1,0:T(8,128)S(1)} %get-tuple-element.48), channel_id=1, source_target_pairs={{0,2},{1,3},{2,0},{3,1},{4,6},{5,7},{6,4},{7,5},{8,10},{9,11},{10,... | collective-permute-start | bytes 196616 | tf_op jit(solution)/shard_map/ppermute | solution.py:76
  101.8 9.1 %collective-permute-start.37 = (f32[64,256]{1,0:T(8,128)S(1)}, f32[64,256]{1,0:T(8,128)S(1)}, u32[]{:S(2)}, u32[]{:S(2)}) collective-permute-start(f32[64,256]{1,0:T(8,128)S(1)} %get-tuple-element.49), channel_id=1, source_target_pairs={{0,3},{1,2},{2,1},{3,0},{4,7},{5,6},{6,5},{7,4},{8,11},{9,10},{10,... | collective-permute-start | bytes 196616 | tf_op jit(solution)/shard_map/ppermute | solution.py:76
  (4 other events, 2.6 us)
where the time goes:
time: 112 us
  starting transfers between devices  52.7 us (47%)
  waiting for transfers between devices  25.7 us (23%)
  Pallas kernels  16.7 us (15%)
  local copies, waits for them, and re-layouts  15.2 us (14%)
    ppermute x26, starting transfers between devices, hop(): lax.ppermute(array, axis, [(mate(i, step, count), i) for i in range(count)])  39.5 us
    ppermute x26, waiting for transfers between devices, hop(): lax.ppermute(array, axis, [(mate(i, step, count), i) for i in range(count)])  18 us
    pallas_call x4, Pallas kernels, call(): pl.pallas_call(kernel, out_shape=outs, in_specs=[SMEM] + [VMEM] * (len(op...  16.7 us
    unnamed x60, local copies, waits for them, and re-layouts  13.5 us
    ppermute x9, starting transfers between devices, sent_to(): lax.ppermute(arrays[j], axis, [(i, mate(i, j, count)) for i in range(coun...  11.1 us
    ppermute x9, waiting for transfers between devices, sent_to(): lax.ppermute(arrays[j], axis, [(i, mate(i, j, count)) for i in range(coun...  7.66 us
  transfers between devices with their start and end apart: 38, of which 10 were waited for; matrix products, arithmetic and copies ran while one was open for 0% of the time, Pallas kernels for 4%

commit v1 on v0

--- a/solution.py
+++ b/solution.py
@@ -368,17 +368,17 @@
 
 VMEM = pl.BlockSpec(memory_space=pltpu.VMEM)
 SMEM = pl.BlockSpec(memory_space=pltpu.SMEM)
-PARAMS = pltpu.CompilerParams(vmem_limit_bytes=48 * 1024 * 1024)
-
-
-def call(kernel, outs, operands, scratch=()):
+MIB = 1024 * 1024
+
+
+def call(kernel, outs, operands, scratch=(), mib=16):
     return pl.pallas_call(
         kernel,
         out_shape=outs,
         in_specs=[SMEM] + [VMEM] * (len(operands) - 1),
         out_specs=jax.tree.map(lambda unused: VMEM, outs),
         scratch_shapes=list(scratch),
-        compiler_params=PARAMS,
+        compiler_params=pltpu.CompilerParams(vmem_limit_bytes=mib * MIB),
     )(*operands)
 
 
@@ -460,6 +460,7 @@
         + (jax.ShapeDtypeStruct((part, 2 * hd), F32),) * dps,
         (place, *inner_all, *outer_all, w1_init[0], w2_init[0]),
         scratch,
+        14 + 2 * blocks,
     )
     got = peers_of(result, "head")
     unused, *d_inner = lax.optimization_barrier((got[1], *d_inner))

time: 112 us -> 112 us (level)
  no operation moved by 1% of the time
where the time goes in v1:
time: 112 us
  starting transfers between devices  52.7 us (47%)
  waiting for transfers between devices  25.7 us (23%)
  Pallas kernels  16.7 us (15%)
  local copies, waits for them, and re-layouts  15.2 us (14%)
    ppermute x26, starting transfers between devices, hop(): lax.ppermute(array, axis, [(mate(i, step, count), i) for i in range(count)])  39.5 us
    ppermute x26, waiting for transfers between devices, hop(): lax.ppermute(array, axis, [(mate(i, step, count), i) for i in range(count)])  18.1 us
    pallas_call x4, Pallas kernels, call(): pl.pallas_call(kernel, out_shape=outs, in_specs=[SMEM] + [VMEM] * (len(op...  16.7 us
    unnamed x60, local copies, waits for them, and re-layouts  13.5 us
    ppermute x9, starting transfers between devices, sent_to(): lax.ppermute(arrays[j], axis, [(i, mate(i, j, count)) for i in range(coun...  11.1 us
    ppermute x9, waiting for transfers between devices, sent_to(): lax.ppermute(arrays[j], axis, [(i, mate(i, j, count)) for i in range(coun...  7.65 us
  transfers between devices with their start and end apart: 38, of which 10 were waited for; matrix products, arithmetic and copies ran while one was open for 0% of the time, Pallas kernels for 4%

profile of v1, /device:TPU:0, one launch (start us, length us, event | category | flops | bytes accessed | tf_op | source)
XLA Modules:
  0.0 111.6 jit_solution(12688925668953363790)
XLA Ops:
  0.7 1.1 fusion.2
  1.8 0.8 collective-permute-start
  2.7 0.7 collective-permute-start.1
  3.4 3.0 %collective-permute-start.2 = (bf16[528,128]{1,0:T(8,128)(2,1)S(1)}, bf16[528,128]{1,0:T(8,128)(2,1)S(1)}, u32[]{:S(2)}, u32[]{:S(2)}) collective-permute-start(bf16[528,128]{1,0:T(8,128)(2,1)S(1)} %collective-permute-done.1.refs_0_.refs_4_), channel_id=1, source_target_pairs={{1,0},{0,1},{3,2},{2,3},{5,4},{4,5},{7,6},{6,7},{9,8},{8,9},{11,10... | collective-permute-start | bytes 405512 | tf_op jit(solution)/shard_map/ppermute | solution.py:65
  6.4 16.6 %collective-permute-start.3 = (bf16[528,128]{1,0:T(8,128)(2,1)S(1)}, bf16[528,128]{1,0:T(8,128)(2,1)S(1)}, u32[]{:S(2)}, u32[]{:S(2)}) collective-permute-start(bf16[528,128]{1,0:T(8,128)(2,1)S(1)} %collective-permute-done.1.refs_0_.refs_4_), channel_id=1, source_target_pairs={{2,0},{3,1},{0,2},{1,3},{6,4},{7,5},{4,6},{5,7},{10,8},{11,9},{8,1... | collective-permute-start | bytes 405512 | tf_op jit(solution)/shard_map/ppermute | solution.py:65
  23.0 0.7 collective-permute-start.16
  23.7 1.3 %collective-permute-start.4 = (bf16[528,128]{1,0:T(8,128)(2,1)S(1)}, bf16[528,128]{1,0:T(8,128)(2,1)S(1)}, u32[]{:S(2)}, u32[]{:S(2)}) collective-permute-start(bf16[528,128]{1,0:T(8,128)(2,1)S(1)} %collective-permute-done.1.refs_0_.refs_4_), channel_id=1, source_target_pairs={{3,0},{2,1},{1,2},{0,3},{7,4},{6,5},{5,6},{4,7},{11,8},{10,9},{9,1... | collective-permute-start | bytes 405512 | tf_op jit(solution)/shard_map/ppermute | solution.py:65
  25.0 1.5 %collective-permute-start.9 = (bf16[768,128]{1,0:T(8,128)(2,1)S(1)}, bf16[768,128]{1,0:T(8,128)(2,1)S(1)}, u32[]{:S(2)}, u32[]{:S(2)}) collective-permute-start(bf16[768,128]{1,0:T(8,128)(2,1)S(1)} %collective-permute-done.refs_0_.refs_12_), channel_id=1, source_target_pairs={{1,0},{0,1},{3,2},{2,3},{5,4},{4,5},{7,6},{6,7},{9,8},{8,9},{11,10... | collective-permute-start | bytes 589832 | tf_op jit(solution)/shard_map/ppermute | solution.py:65
  26.4 0.8 collective-permute-start.10
  27.2 0.6 collective-permute-start.5
  27.9 0.7 copy-done.2
  28.5 2.2 %collective-permute-done.4.refs_3_.refs_7_ = bf16[528,128]{1,0:T(8,128)(2,1)S(1)} collective-permute-done((bf16[528,128]{1,0:T(8,128)(2,1)S(1)}, bf16[528,128]{1,0:T(8,128)(2,1)S(1)}, u32[]{:S(2)}, u32[]{:S(2)}) %collective-permute-start.4) | collective-permute-done | bytes 135200 | tf_op jit(solution)/shard_map/ppermute | solution.py:65
  30.7 0.6 collective-permute-start.12
  31.4 4.9 %collective-permute-start.18 = (bf16[768,128]{1,0:T(8,128)(2,1)S(1)}, bf16[768,128]{1,0:T(8,128)(2,1)S(1)}, u32[]{:S(2)}, u32[]{:S(2)}) collective-permute-start(bf16[768,128]{1,0:T(8,128)(2,1)S(1)} %collective-permute-done.16.refs_8_.refs_20_), channel_id=1, source_target_pairs={{2,0},{3,1},{0,2},{1,3},{6,4},{7,5},{4,6},{5,7},{10,8},{11,9},{8,1... | collective-permute-start | bytes 589832 | tf_op jit(solution)/shard_map/ppermute | solution.py:65
  36.2 0.7 copy-done.14
  36.9 0.7 copy-done.5
  37.6 0.5 collective-permute-start.7
  38.1 0.7 copy-done.8
  38.7 0.7 copy-done.11
  39.4 1.8 %collective-permute-start.11 = (bf16[768,128]{1,0:T(8,128)(2,1)S(1)}, bf16[768,128]{1,0:T(8,128)(2,1)S(1)}, u32[]{:S(2)}, u32[]{:S(2)}) collective-permute-start(bf16[768,128]{1,0:T(8,128)(2,1)S(1)} %collective-permute-done.9.refs_1_.refs_13_), channel_id=1, source_target_pairs={{2,0},{3,1},{0,2},{1,3},{6,4},{7,5},{4,6},{5,7},{10,8},{11,9},{8,1... | collective-permute-start | bytes 589832 | tf_op jit(solution)/shard_map/ppermute | solution.py:65
  41.2 0.7 copy-done.17
  41.8 0.1 collective-permute-start.13
  41.9 0.6 copy-done.20
  42.5 0.6 collective-permute-start.17
  43.1 0.7 copy-done.23
  43.8 1.6 %collective-permute-start.19 = (bf16[768,128]{1,0:T(8,128)(2,1)S(1)}, bf16[768,128]{1,0:T(8,128)(2,1)S(1)}, u32[]{:S(2)}, u32[]{:S(2)}) collective-permute-start(bf16[768,128]{1,0:T(8,128)(2,1)S(1)} %collective-permute-done.18.refs_10_.refs_22_), channel_id=1, source_target_pairs={{1,0},{0,1},{3,2},{2,3},{5,4},{4,5},{7,6},{6,7},{9,8},{8,9},{11,10... | collective-permute-start | bytes 589832 | tf_op jit(solution)/shard_map/ppermute | solution.py:65
  45.4 1.3 %collective-permute-done.11.refs_3_.refs_15_ = bf16[768,128]{1,0:T(8,128)(2,1)S(1)} collective-permute-done((bf16[768,128]{1,0:T(8,128)(2,1)S(1)}, bf16[768,128]{1,0:T(8,128)(2,1)S(1)}, u32[]{:S(2)}, u32[]{:S(2)}) %collective-permute-start.11) | collective-permute-done | bytes 196640 | tf_op jit(solution)/shard_map/ppermute | solution.py:65
  46.7 0.5 collective-permute-start.22
  47.2 3.0 %collective-permute-done.17.refs_9_.refs_21_ = bf16[768,128]{1,0:T(8,128)(2,1)S(1)} collective-permute-done((bf16[768,128]{1,0:T(8,128)(2,1)S(1)}, bf16[768,128]{1,0:T(8,128)(2,1)S(1)}, u32[]{:S(2)}, u32[]{:S(2)}) %collective-permute-start.17) | collective-permute-done | bytes 196640 | tf_op jit(solution)/shard_map/ppermute | solution.py:65
  50.3 0.5 collective-permute-start.21
  50.8 3.2 %collective-permute-done.19.refs_11_.refs_23_ = bf16[768,128]{1,0:T(8,128)(2,1)S(1)} collective-permute-done((bf16[768,128]{1,0:T(8,128)(2,1)S(1)}, bf16[768,128]{1,0:T(8,128)(2,1)S(1)}, u32[]{:S(2)}, u32[]{:S(2)}) %collective-permute-start.19) | collective-permute-done | bytes 196640 | tf_op jit(solution)/shard_map/ppermute | solution.py:65
  54.0 0.1 pad_add_fusion.place_ref
  54.1 0.9 copy-done.3
  55.0 0.9 copy-done.6
  55.9 0.9 copy-done.9
  56.8 0.9 copy-done.12
  57.7 0.9 copy-done.15
  58.6 0.9 copy-done.18
  59.5 0.9 copy-done.21
  60.4 0.9 copy-done.24
  61.3 0.9 copy-done.26
  62.3 1.3 %shard_map.102 = (bf16[144,128]{1,0:T(8,128)(2,1)S(1)}, bf16[144,128]{1,0:T(8,128)(2,1)S(1)}, bf16[144,128]{1,0:T(8,128)(2,1)S(1)}, bf16[144,128]{1,0:T(8,128)(2,1)S(1)}) custom-call(s32[3]{0:T(128)S(1)} %pad_add_fusion.place_ref, bf16[128,1024]{1,0:T(8,128)(2,1)S(1)} %bitcast.21, bf16[128,1024]{1,0:T(8,128)(2,1)S(1)} %bitcast.23, ...), custom_call_target="tpu_custom_call" | custom-call | tf_op jit(solution)/shard_map/pallas_call | solution.py:375
  63.6 1.4 %shard_map.103 = (bf16[128,384]{1,0:T(8,128)(2,1)S(1)}, bf16[128,384]{1,0:T(8,128)(2,1)S(1)}, bf16[128,384]{1,0:T(8,128)(2,1)S(1)}, bf16[128,384]{1,0:T(8,128)(2,1)S(1)}) custom-call(s32[3]{0:T(128)S(1)} %pad_add_fusion.place_ref, bf16[128,1024]{1,0:T(8,128)(2,1)S(1)} %bitcast.22, bf16[768,128]{1,0:T(8,128)(2,1)S(1)} %collective-permute-done.refs_0_.refs_12_, ...), custom_call_target="tpu_custom_call" | custom-call | tf_op jit(solution)/shard_map/pallas_call | solution.py:375
  65.0 0.1 collective-permute-start.24
  65.1 0.7 collective-permute-start.25
  65.8 3.6 %collective-permute-start.26 = (bf16[128,384]{1,0:T(8,128)(2,1)S(1)}, bf16[128,384]{1,0:T(8,128)(2,1)S(1)}, u32[]{:S(2)}, u32[]{:S(2)}) collective-permute-start(bf16[128,384]{1,0:T(8,128)(2,1)S(1)} %get-tuple-element.35), channel_id=1, source_target_pairs={{0,12},{4,8},{8,4},{12,0},{1,13},{5,9},{9,5},{13,1},{2,14},{6,10},... | collective-permute-start | bytes 294920 | tf_op jit(solution)/shard_map/ppermute | solution.py:76
  69.5 0.7 collective-permute-start.29
  70.2 1.2 %collective-permute-done.24 = bf16[128,384]{1,0:T(8,128)(2,1)S(1)} collective-permute-done((bf16[128,384]{1,0:T(8,128)(2,1)S(1)}, bf16[128,384]{1,0:T(8,128)(2,1)S(1)}, u32[]{:S(2)}, u32[]{:S(2)}) %collective-permute-start.24) | collective-permute-done | bytes 98336 | tf_op jit(solution)/shard_map/ppermute | solution.py:76
  71.4 2.4 %collective-permute-start.30 = (bf16[144,128]{1,0:T(8,128)(2,1)S(1)}, bf16[144,128]{1,0:T(8,128)(2,1)S(1)}, u32[]{:S(2)}, u32[]{:S(2)}) collective-permute-start(bf16[144,128]{1,0:T(8,128)(2,1)S(1)} %get-tuple-element.38), channel_id=1, source_target_pairs={{0,12},{4,8},{8,4},{12,0},{1,13},{5,9},{9,5},{13,1},{2,14},{6,10},... | collective-permute-start | bytes 110600 | tf_op jit(solution)/shard_map/ppermute | solution.py:76
  73.9 3.7 %collective-permute-done.25 = bf16[128,384]{1,0:T(8,128)(2,1)S(1)} collective-permute-done((bf16[128,384]{1,0:T(8,128)(2,1)S(1)}, bf16[128,384]{1,0:T(8,128)(2,1)S(1)}, u32[]{:S(2)}, u32[]{:S(2)}) %collective-permute-start.25) | collective-permute-done | bytes 98336 | tf_op jit(solution)/shard_map/ppermute | solution.py:76
  77.7 2.7 %collective-permute-done.29 = bf16[144,128]{1,0:T(8,128)(2,1)S(1)} collective-permute-done((bf16[144,128]{1,0:T(8,128)(2,1)S(1)}, bf16[144,128]{1,0:T(8,128)(2,1)S(1)}, u32[]{:S(2)}, u32[]{:S(2)}) %collective-permute-start.29) | collective-permute-done | bytes 36896 | tf_op jit(solution)/shard_map/ppermute | solution.py:76
  80.5 0.1 collective-permute-start.31
  80.5 1.3 %collective-permute-done.31.refs_3_ = f32[144,128]{1,0:T(8,128)S(1)} collective-permute-done((f32[144,128]{1,0:T(8,128)S(1)}, f32[144,128]{1,0:T(8,128)S(1)}, u32[]{:S(2)}, u32[]{:S(2)}) %collective-permute-start.31) | collective-permute-done | bytes 73760 | tf_op jit(solution)/shard_map/ppermute | solution.py:65
  81.9 10.9 %shard_map.104 = (bf16[144,512]{1,0:T(8,128)(2,1)S(1)}, f32[64,256]{1,0:T(8,128)S(1)}, f32[64,256]{1,0:T(8,128)S(1)}, f32[64,256]{1,0:T(8,128)S(1)}, f32[64,256]{1,0:T(8,128)S(1)}) custom-call(s32[3]{0:T(128)S(1)} %pad_add_fusion.place_ref, f32[128,384]{1,0:T(8,128)S(1)} %convert_add_fusion.refs_0_, f32[128,384]{1,0:T(8,128)S(1)} %collective-permute-done.27.refs_1_, ...), custom_call_target="tpu_custom_call" | custom-call | tf_op jit(solution)/shard_map/pallas_call | solution.py:375
  92.7 1.0 collective-permute-start.32
  93.8 0.9 collective-permute-start.33
  94.7 2.5 %collective-permute-start.34 = (bf16[144,512]{1,0:T(8,128)(2,1)S(1)}, bf16[144,512]{1,0:T(8,128)(2,1)S(1)}, u32[]{:S(2)}, u32[]{:S(2)}) collective-permute-start(bf16[144,512]{1,0:T(8,128)(2,1)S(1)} %get-tuple-element.39.refs_0_), channel_id=1, source_target_pairs={{12,0},{8,4},{4,8},{0,12},{13,1},{9,5},{5,9},{1,13},{14,2},{10,6},... | collective-permute-start | bytes 442376 | tf_op jit(solution)/shard_map/ppermute | solution.py:65
  97.2 3.3 %collective-permute-done.32.refs_1_ = bf16[144,512]{1,0:T(8,128)(2,1)S(1)} collective-permute-done((bf16[144,512]{1,0:T(8,128)(2,1)S(1)}, bf16[144,512]{1,0:T(8,128)(2,1)S(1)}, u32[]{:S(2)}, u32[]{:S(2)}) %collective-permute-start.32) | collective-permute-done | bytes 147488 | tf_op jit(solution)/shard_map/ppermute | solution.py:65
  100.5 0.6 collective-permute-start.35
  101.0 0.7 collective-permute-start.36
  101.8 2.2 %collective-permute-start.37 = (f32[64,256]{1,0:T(8,128)S(1)}, f32[64,256]{1,0:T(8,128)S(1)}, u32[]{:S(2)}, u32[]{:S(2)}) collective-permute-start(f32[64,256]{1,0:T(8,128)S(1)} %get-tuple-element.49), channel_id=1, source_target_pairs={{0,3},{1,2},{2,1},{3,0},{4,7},{5,6},{6,5},{7,4},{8,11},{9,10},{10,... | collective-permute-start | bytes 196616 | tf_op jit(solution)/shard_map/ppermute | solution.py:76
  104.0 3.7 %collective-permute-done.33.refs_2_ = bf16[144,512]{1,0:T(8,128)(2,1)S(1)} collective-permute-done((bf16[144,512]{1,0:T(8,128)(2,1)S(1)}, bf16[144,512]{1,0:T(8,128)(2,1)S(1)}, u32[]{:S(2)}, u32[]{:S(2)}) %collective-permute-start.33) | collective-permute-done | bytes 147488 | tf_op jit(solution)/shard_map/ppermute | solution.py:65
  107.8 3.2 %shard_map.105 = (bf16[128,1024]{1,0:T(8,128)(2,1)}, bf16[128,1024]{1,0:T(8,128)(2,1)}) custom-call(s32[3]{0:T(128)S(1)} %pad_add_fusion.place_ref, bf16[144,512]{1,0:T(8,128)(2,1)S(1)} %get-tuple-element.39.refs_0_, bf16[144,512]{1,0:T(8,128)(2,1)S(1)} %collective-permute-done.32.refs_1_, bf16[144,512]{1,0:T(8,128)(2,1)S(1)} %collective-permute-done.33.refs_2_, ...), custom_call_target="tpu_custom_call" | custom-call | tf_op jit(solution)/shard_map/pallas_call | solution.py:375
  111.0 0.6 slice_bitcast_fusion
  (85 shorter events, 0.5 us)
Async XLA Ops:
  0.6 2.0 %copy-start = (bf16[4096,1]{0,1:T(2,128)(2,1)S(1)}, bf16[4096,1]{0,1:T(2,128)(2,1)}, u32[]{:S(2)}) copy-start(bf16[4096,1]{0,1:T(2,128)(2,1)} %param.9) | copy-start | bytes 24580
  0.6 2.0 %copy-start.29 = (bf16[512,128]{1,0:T(8,128)(2,1)S(1)}, bf16[512,128]{1,0:T(8,128)(2,1)}, u32[]{:S(2)}) copy-start(bf16[512,128]{1,0:T(8,128)(2,1)} %param.10) | copy-start | bytes 393220
  1.7 52.3 %copy-start.1 = (bf16[1,128,1024]{2,1,0:T(8,128)(2,1)S(1)}, bf16[1,128,1024]{2,1,0:T(8,128)(2,1)}, u32[]{:S(2)}) copy-start(bf16[1,128,1024]{2,1,0:T(8,128)(2,1)} %param.7) | copy-start | bytes 786436
  1.8 1.6 %collective-permute-start = (bf16[768,128]{1,0:T(8,128)(2,1)S(1)}, bf16[768,128]{1,0:T(8,128)(2,1)S(1)}, u32[]{:S(2)}, u32[]{:S(2)}) collective-permute-start(bf16[768,128]{1,0:T(8,128)(2,1)S(1)} %bitcast.28), channel_id=1, source_target_pairs={{0,0},{1,1},{2,4},{3,5},{4,2},{5,3},{6,6},{7,7},{8,16},{9,17},{10,... | collective-permute-start | bytes 589832 | tf_op jit(solution)/shard_map/ppermute | solution.py:405
  2.7 0.7 collective-permute-start.1
  3.4 23.1 %collective-permute-start.2 = (bf16[528,128]{1,0:T(8,128)(2,1)S(1)}, bf16[528,128]{1,0:T(8,128)(2,1)S(1)}, u32[]{:S(2)}, u32[]{:S(2)}) collective-permute-start(bf16[528,128]{1,0:T(8,128)(2,1)S(1)} %collective-permute-done.1.refs_0_.refs_4_), channel_id=1, source_target_pairs={{1,0},{0,1},{3,2},{2,3},{5,4},{4,5},{7,6},{6,7},{9,8},{8,9},{11,10... | collective-permute-start | bytes 405512 | tf_op jit(solution)/shard_map/ppermute | solution.py:65
  6.4 20.8 %collective-permute-start.3 = (bf16[528,128]{1,0:T(8,128)(2,1)S(1)}, bf16[528,128]{1,0:T(8,128)(2,1)S(1)}, u32[]{:S(2)}, u32[]{:S(2)}) collective-permute-start(bf16[528,128]{1,0:T(8,128)(2,1)S(1)} %collective-permute-done.1.refs_0_.refs_4_), channel_id=1, source_target_pairs={{2,0},{3,1},{0,2},{1,3},{6,4},{7,5},{4,6},{5,7},{10,8},{11,9},{8,1... | collective-permute-start | bytes 405512 | tf_op jit(solution)/shard_map/ppermute | solution.py:65
  23.0 8.4 %collective-permute-start.16 = (bf16[768,128]{1,0:T(8,128)(2,1)S(1)}, bf16[768,128]{1,0:T(8,128)(2,1)S(1)}, u32[]{:S(2)}, u32[]{:S(2)}) collective-permute-start(bf16[768,128]{1,0:T(8,128)(2,1)S(1)} %bitcast.27), channel_id=1, source_target_pairs={{0,0},{1,1},{2,4},{3,5},{4,2},{5,3},{6,6},{7,7},{8,16},{9,17},{10,... | collective-permute-start | bytes 589832 | tf_op jit(solution)/shard_map/ppermute | solution.py:405
  23.7 7.0 %collective-permute-start.4 = (bf16[528,128]{1,0:T(8,128)(2,1)S(1)}, bf16[528,128]{1,0:T(8,128)(2,1)S(1)}, u32[]{:S(2)}, u32[]{:S(2)}) collective-permute-start(bf16[528,128]{1,0:T(8,128)(2,1)S(1)} %collective-permute-done.1.refs_0_.refs_4_), channel_id=1, source_target_pairs={{3,0},{2,1},{1,2},{0,3},{7,4},{6,5},{5,6},{4,7},{11,8},{10,9},{9,1... | collective-permute-start | bytes 405512 | tf_op jit(solution)/shard_map/ppermute | solution.py:65
  25.0 12.6 %collective-permute-start.9 = (bf16[768,128]{1,0:T(8,128)(2,1)S(1)}, bf16[768,128]{1,0:T(8,128)(2,1)S(1)}, u32[]{:S(2)}, u32[]{:S(2)}) collective-permute-start(bf16[768,128]{1,0:T(8,128)(2,1)S(1)} %collective-permute-done.refs_0_.refs_12_), channel_id=1, source_target_pairs={{1,0},{0,1},{3,2},{2,3},{5,4},{4,5},{7,6},{6,7},{9,8},{8,9},{11,10... | collective-permute-start | bytes 589832 | tf_op jit(solution)/shard_map/ppermute | solution.py:65
  26.4 12.3 %collective-permute-start.10 = (bf16[768,128]{1,0:T(8,128)(2,1)S(1)}, bf16[768,128]{1,0:T(8,128)(2,1)S(1)}, u32[]{:S(2)}, u32[]{:S(2)}) collective-permute-start(bf16[768,128]{1,0:T(8,128)(2,1)S(1)} %collective-permute-done.refs_0_.refs_12_), channel_id=1, source_target_pairs={{2,0},{3,1},{0,2},{1,3},{6,4},{7,5},{4,6},{5,7},{10,8},{11,9},{8,1... | collective-permute-start | bytes 589832 | tf_op jit(solution)/shard_map/ppermute | solution.py:65
  27.2 9.0 %collective-permute-start.5 = (bf16[528,128]{1,0:T(8,128)(2,1)S(1)}, bf16[528,128]{1,0:T(8,128)(2,1)S(1)}, u32[]{:S(2)}, u32[]{:S(2)}) collective-permute-start(bf16[528,128]{1,0:T(8,128)(2,1)S(1)} %collective-permute-done.1.refs_0_.refs_4_), channel_id=1, source_target_pairs={{16,0},{0,16},{17,1},{1,17},{18,2},{2,18},{19,3},{3,19},{20,4},{4,... | collective-permute-start | bytes 405512 | tf_op jit(solution)/shard_map/ppermute | solution.py:65
  30.7 8.7 %collective-permute-start.12 = (bf16[768,128]{1,0:T(8,128)(2,1)S(1)}, bf16[768,128]{1,0:T(8,128)(2,1)S(1)}, u32[]{:S(2)}, u32[]{:S(2)}) collective-permute-start(bf16[768,128]{1,0:T(8,128)(2,1)S(1)} %collective-permute-done.refs_0_.refs_12_), channel_id=1, source_target_pairs={{16,0},{0,16},{17,1},{1,17},{18,2},{2,18},{19,3},{3,19},{20,4},{4,... | collective-permute-start | bytes 589832 | tf_op jit(solution)/shard_map/ppermute | solution.py:65
  31.4 12.5 %collective-permute-start.18 = (bf16[768,128]{1,0:T(8,128)(2,1)S(1)}, bf16[768,128]{1,0:T(8,128)(2,1)S(1)}, u32[]{:S(2)}, u32[]{:S(2)}) collective-permute-start(bf16[768,128]{1,0:T(8,128)(2,1)S(1)} %collective-permute-done.16.refs_8_.refs_20_), channel_id=1, source_target_pairs={{2,0},{3,1},{0,2},{1,3},{6,4},{7,5},{4,6},{5,7},{10,8},{11,9},{8,1... | collective-permute-start | bytes 589832 | tf_op jit(solution)/shard_map/ppermute | solution.py:65
  36.9 4.3 %collective-permute-start.6 = (bf16[528,128]{1,0:T(8,128)(2,1)S(1)}, bf16[528,128]{1,0:T(8,128)(2,1)S(1)}, u32[]{:S(2)}, u32[]{:S(2)}) collective-permute-start(bf16[528,128]{1,0:T(8,128)(2,1)S(1)} %collective-permute-done.2.refs_1_.refs_5_), channel_id=1, source_target_pairs={{16,0},{0,16},{17,1},{1,17},{18,2},{2,18},{19,3},{3,19},{20,4},{4,... | collective-permute-start | bytes 405512 | tf_op jit(solution)/shard_map/ppermute | solution.py:65
  36.9 0.7 copy-start.5
  37.6 4.3 %collective-permute-start.7 = (bf16[528,128]{1,0:T(8,128)(2,1)S(1)}, bf16[528,128]{1,0:T(8,128)(2,1)S(1)}, u32[]{:S(2)}, u32[]{:S(2)}) collective-permute-start(bf16[528,128]{1,0:T(8,128)(2,1)S(1)} %collective-permute-done.3.refs_2_.refs_6_), channel_id=1, source_target_pairs={{16,0},{0,16},{17,1},{1,17},{18,2},{2,18},{19,3},{3,19},{20,4},{4,... | collective-permute-start | bytes 405512 | tf_op jit(solution)/shard_map/ppermute | solution.py:65
  38.7 4.4 %collective-permute-start.8 = (bf16[528,128]{1,0:T(8,128)(2,1)S(1)}, bf16[528,128]{1,0:T(8,128)(2,1)S(1)}, u32[]{:S(2)}, u32[]{:S(2)}) collective-permute-start(bf16[528,128]{1,0:T(8,128)(2,1)S(1)} %collective-permute-done.4.refs_3_.refs_7_), channel_id=1, source_target_pairs={{16,0},{0,16},{17,1},{1,17},{18,2},{2,18},{19,3},{3,19},{20,4},{4,... | collective-permute-start | bytes 405512 | tf_op jit(solution)/shard_map/ppermute | solution.py:65
  38.7 0.7 copy-start.11
  39.4 7.3 %collective-permute-start.11 = (bf16[768,128]{1,0:T(8,128)(2,1)S(1)}, bf16[768,128]{1,0:T(8,128)(2,1)S(1)}, u32[]{:S(2)}, u32[]{:S(2)}) collective-permute-start(bf16[768,128]{1,0:T(8,128)(2,1)S(1)} %collective-permute-done.9.refs_1_.refs_13_), channel_id=1, source_target_pairs={{2,0},{3,1},{0,2},{1,3},{6,4},{7,5},{4,6},{5,7},{10,8},{11,9},{8,1... | collective-permute-start | bytes 589832 | tf_op jit(solution)/shard_map/ppermute | solution.py:65
  41.1 0.7 copy-start.17
  41.8 4.9 %collective-permute-start.13 = (bf16[768,128]{1,0:T(8,128)(2,1)S(1)}, bf16[768,128]{1,0:T(8,128)(2,1)S(1)}, u32[]{:S(2)}, u32[]{:S(2)}) collective-permute-start(bf16[768,128]{1,0:T(8,128)(2,1)S(1)} %collective-permute-done.9.refs_1_.refs_13_), channel_id=1, source_target_pairs={{16,0},{0,16},{17,1},{1,17},{18,2},{2,18},{19,3},{3,19},{20,4},{4,... | collective-permute-start | bytes 589832 | tf_op jit(solution)/shard_map/ppermute | solution.py:65
  42.5 7.7 %collective-permute-start.17 = (bf16[768,128]{1,0:T(8,128)(2,1)S(1)}, bf16[768,128]{1,0:T(8,128)(2,1)S(1)}, u32[]{:S(2)}, u32[]{:S(2)}) collective-permute-start(bf16[768,128]{1,0:T(8,128)(2,1)S(1)} %collective-permute-done.16.refs_8_.refs_20_), channel_id=1, source_target_pairs={{1,0},{0,1},{3,2},{2,3},{5,4},{4,5},{7,6},{6,7},{9,8},{8,9},{11,10... | collective-permute-start | bytes 589832 | tf_op jit(solution)/shard_map/ppermute | solution.py:65
  43.1 0.7 copy-start.23
  43.8 6.5 %collective-permute-start.14 = (bf16[768,128]{1,0:T(8,128)(2,1)S(1)}, bf16[768,128]{1,0:T(8,128)(2,1)S(1)}, u32[]{:S(2)}, u32[]{:S(2)}) collective-permute-start(bf16[768,128]{1,0:T(8,128)(2,1)S(1)} %collective-permute-done.10.refs_2_.refs_14_), channel_id=1, source_target_pairs={{16,0},{0,16},{17,1},{1,17},{18,2},{2,18},{19,3},{3,19},{20,4},{4,... | collective-permute-start | bytes 589832 | tf_op jit(solution)/shard_map/ppermute | solution.py:65
  43.8 10.2 %collective-permute-start.19 = (bf16[768,128]{1,0:T(8,128)(2,1)S(1)}, bf16[768,128]{1,0:T(8,128)(2,1)S(1)}, u32[]{:S(2)}, u32[]{:S(2)}) collective-permute-start(bf16[768,128]{1,0:T(8,128)(2,1)S(1)} %collective-permute-done.18.refs_10_.refs_22_), channel_id=1, source_target_pairs={{1,0},{0,1},{3,2},{2,3},{5,4},{4,5},{7,6},{6,7},{9,8},{8,9},{11,10... | collective-permute-start | bytes 589832 | tf_op jit(solution)/shard_map/ppermute | solution.py:65
  46.7 16.9 %collective-permute-start.20 = (bf16[768,128]{1,0:T(8,128)(2,1)S(1)}, bf16[768,128]{1,0:T(8,128)(2,1)S(1)}, u32[]{:S(2)}, u32[]{:S(2)}) collective-permute-start(bf16[768,128]{1,0:T(8,128)(2,1)S(1)} %collective-permute-done.16.refs_8_.refs_20_), channel_id=1, source_target_pairs={{16,0},{0,16},{17,1},{1,17},{18,2},{2,18},{19,3},{3,19},{20,4},{4,... | collective-permute-start | bytes 589832 | tf_op jit(solution)/shard_map/ppermute | solution.py:65
  46.7 16.9 %collective-permute-start.22 = (bf16[768,128]{1,0:T(8,128)(2,1)S(1)}, bf16[768,128]{1,0:T(8,128)(2,1)S(1)}, u32[]{:S(2)}, u32[]{:S(2)}) collective-permute-start(bf16[768,128]{1,0:T(8,128)(2,1)S(1)} %collective-permute-done.18.refs_10_.refs_22_), channel_id=1, source_target_pairs={{16,0},{0,16},{17,1},{1,17},{18,2},{2,18},{19,3},{3,19},{20,4},{4,... | collective-permute-start | bytes 589832 | tf_op jit(solution)/shard_map/ppermute | solution.py:65
  50.3 13.3 %collective-permute-start.15 = (bf16[768,128]{1,0:T(8,128)(2,1)S(1)}, bf16[768,128]{1,0:T(8,128)(2,1)S(1)}, u32[]{:S(2)}, u32[]{:S(2)}) collective-permute-start(bf16[768,128]{1,0:T(8,128)(2,1)S(1)} %collective-permute-done.11.refs_3_.refs_15_), channel_id=1, source_target_pairs={{16,0},{0,16},{17,1},{1,17},{18,2},{2,18},{19,3},{3,19},{20,4},{4,... | collective-permute-start | bytes 589832 | tf_op jit(solution)/shard_map/ppermute | solution.py:65
  50.3 13.4 %collective-permute-start.21 = (bf16[768,128]{1,0:T(8,128)(2,1)S(1)}, bf16[768,128]{1,0:T(8,128)(2,1)S(1)}, u32[]{:S(2)}, u32[]{:S(2)}) collective-permute-start(bf16[768,128]{1,0:T(8,128)(2,1)S(1)} %collective-permute-done.17.refs_9_.refs_21_), channel_id=1, source_target_pairs={{16,0},{0,16},{17,1},{1,17},{18,2},{2,18},{19,3},{3,19},{20,4},{4,... | collective-permute-start | bytes 589832 | tf_op jit(solution)/shard_map/ppermute | solution.py:65
  54.0 9.6 %collective-permute-start.23 = (bf16[768,128]{1,0:T(8,128)(2,1)S(1)}, bf16[768,128]{1,0:T(8,128)(2,1)S(1)}, u32[]{:S(2)}, u32[]{:S(2)}) collective-permute-start(bf16[768,128]{1,0:T(8,128)(2,1)S(1)} %collective-permute-done.19.refs_11_.refs_23_), channel_id=1, source_target_pairs={{16,0},{0,16},{17,1},{1,17},{18,2},{2,18},{19,3},{3,19},{20,4},{4,... | collective-permute-start | bytes 589832 | tf_op jit(solution)/shard_map/ppermute | solution.py:65
  54.1 0.9 copy-start.3
  55.0 0.9 copy-start.6
  55.9 0.9 copy-start.9
  56.8 0.9 copy-start.12
  57.7 0.9 copy-start.15
  58.6 0.9 copy-start.18
  59.5 0.9 copy-start.21
  60.4 0.9 copy-start.24
  61.3 0.9 copy-start.26
  65.0 6.4 %collective-permute-start.24 = (bf16[128,384]{1,0:T(8,128)(2,1)S(1)}, bf16[128,384]{1,0:T(8,128)(2,1)S(1)}, u32[]{:S(2)}, u32[]{:S(2)}) collective-permute-start(bf16[128,384]{1,0:T(8,128)(2,1)S(1)} %get-tuple-element.33), channel_id=1, source_target_pairs={{0,4},{4,0},{8,12},{12,8},{1,5},{5,1},{9,13},{13,9},{2,6},{6,2},{1... | collective-permute-start | bytes 294920 | tf_op jit(solution)/shard_map/ppermute | solution.py:76
  65.1 12.4 %collective-permute-start.25 = (bf16[128,384]{1,0:T(8,128)(2,1)S(1)}, bf16[128,384]{1,0:T(8,128)(2,1)S(1)}, u32[]{:S(2)}, u32[]{:S(2)}) collective-permute-start(bf16[128,384]{1,0:T(8,128)(2,1)S(1)} %get-tuple-element.34), channel_id=1, source_target_pairs={{0,8},{4,12},{8,0},{12,4},{1,9},{5,13},{9,1},{13,5},{2,10},{6,14},... | collective-permute-start | bytes 294920 | tf_op jit(solution)/shard_map/ppermute | solution.py:76
  65.8 11.7 %collective-permute-start.26 = (bf16[128,384]{1,0:T(8,128)(2,1)S(1)}, bf16[128,384]{1,0:T(8,128)(2,1)S(1)}, u32[]{:S(2)}, u32[]{:S(2)}) collective-permute-start(bf16[128,384]{1,0:T(8,128)(2,1)S(1)} %get-tuple-element.35), channel_id=1, source_target_pairs={{0,12},{4,8},{8,4},{12,0},{1,13},{5,9},{9,5},{13,1},{2,14},{6,10},... | collective-permute-start | bytes 294920 | tf_op jit(solution)/shard_map/ppermute | solution.py:76
  69.5 8.2 %collective-permute-start.28 = (bf16[144,128]{1,0:T(8,128)(2,1)S(1)}, bf16[144,128]{1,0:T(8,128)(2,1)S(1)}, u32[]{:S(2)}, u32[]{:S(2)}) collective-permute-start(bf16[144,128]{1,0:T(8,128)(2,1)S(1)} %get-tuple-element.36), channel_id=1, source_target_pairs={{0,4},{4,0},{8,12},{12,8},{1,5},{5,1},{9,13},{13,9},{2,6},{6,2},{1... | collective-permute-start | bytes 110600 | tf_op jit(solution)/shard_map/ppermute | solution.py:76
  69.5 11.0 %collective-permute-start.29 = (bf16[144,128]{1,0:T(8,128)(2,1)S(1)}, bf16[144,128]{1,0:T(8,128)(2,1)S(1)}, u32[]{:S(2)}, u32[]{:S(2)}) collective-permute-start(bf16[144,128]{1,0:T(8,128)(2,1)S(1)} %get-tuple-element.37), channel_id=1, source_target_pairs={{0,8},{4,12},{8,0},{12,4},{1,9},{5,13},{9,1},{13,5},{2,10},{6,14},... | collective-permute-start | bytes 110600 | tf_op jit(solution)/shard_map/ppermute | solution.py:76
  71.4 9.0 %collective-permute-start.30 = (bf16[144,128]{1,0:T(8,128)(2,1)S(1)}, bf16[144,128]{1,0:T(8,128)(2,1)S(1)}, u32[]{:S(2)}, u32[]{:S(2)}) collective-permute-start(bf16[144,128]{1,0:T(8,128)(2,1)S(1)} %get-tuple-element.38), channel_id=1, source_target_pairs={{0,12},{4,8},{8,4},{12,0},{1,13},{5,9},{9,5},{13,1},{2,14},{6,10},... | collective-permute-start | bytes 110600 | tf_op jit(solution)/shard_map/ppermute | solution.py:76
  77.5 4.3 %copy-start.27 = (f32[1,128,512]{2,1,0:T(8,128)S(1)}, f32[1,128,512]{2,1,0:T(8,128)}, u32[]{:S(2)}) copy-start(f32[1,128,512]{2,1,0:T(8,128)} %param.11) | copy-start | bytes 786436
  77.5 4.3 %copy-start.28 = (f32[1,512,128]{2,1,0:T(8,128)S(1)}, f32[1,512,128]{2,1,0:T(8,128)}, u32[]{:S(2)}) copy-start(f32[1,512,128]{2,1,0:T(8,128)} %param.12) | copy-start | bytes 786436
  77.6 4.2 %collective-permute-start.27 = (f32[128,384]{1,0:T(8,128)S(1)}, f32[128,384]{1,0:T(8,128)S(1)}, u32[]{:S(2)}, u32[]{:S(2)}) collective-permute-start(f32[128,384]{1,0:T(8,128)S(1)} %convert_add_fusion.refs_0_), channel_id=1, source_target_pairs={{16,0},{0,16},{17,1},{1,17},{18,2},{2,18},{19,3},{3,19},{20,4},{4,... | collective-permute-start | bytes 589832 | tf_op jit(solution)/shard_map/ppermute | solution.py:65
  80.4 27.3 %copy-start.25 = (bf16[528,128]{1,0:T(8,128)(2,1)S(1)}, bf16[528,128]{1,0:T(8,128)(2,1)}, u32[]{:S(2)}) copy-start(bf16[528,128]{1,0:T(8,128)(2,1)} %copy-done.23) | copy-start | bytes 405508
  80.5 1.3 %collective-permute-start.31 = (f32[144,128]{1,0:T(8,128)S(1)}, f32[144,128]{1,0:T(8,128)S(1)}, u32[]{:S(2)}, u32[]{:S(2)}) collective-permute-start(f32[144,128]{1,0:T(8,128)S(1)} %convert_add_fusion.1.refs_2_), channel_id=1, source_target_pairs={{16,0},{0,16},{17,1},{1,17},{18,2},{2,18},{19,3},{3,19},{20,4},{4,... | collective-permute-start | bytes 221192 | tf_op jit(solution)/shard_map/ppermute | solution.py:65
  81.8 25.9 %copy-start.4 = (bf16[528,128]{1,0:T(8,128)(2,1)S(1)}, bf16[528,128]{1,0:T(8,128)(2,1)}, u32[]{:S(2)}) copy-start(bf16[528,128]{1,0:T(8,128)(2,1)} %copy-done.2) | copy-start | bytes 405508
  81.8 25.9 %copy-start.7 = (bf16[528,128]{1,0:T(8,128)(2,1)S(1)}, bf16[528,128]{1,0:T(8,128)(2,1)}, u32[]{:S(2)}) copy-start(bf16[528,128]{1,0:T(8,128)(2,1)} %copy-done.5) | copy-start | bytes 405508
  81.8 25.9 %copy-start.10 = (bf16[528,128]{1,0:T(8,128)(2,1)S(1)}, bf16[528,128]{1,0:T(8,128)(2,1)}, u32[]{:S(2)}) copy-start(bf16[528,128]{1,0:T(8,128)(2,1)} %copy-done.8) | copy-start | bytes 405508
  81.8 25.9 %copy-start.13 = (bf16[528,128]{1,0:T(8,128)(2,1)S(1)}, bf16[528,128]{1,0:T(8,128)(2,1)}, u32[]{:S(2)}) copy-start(bf16[528,128]{1,0:T(8,128)(2,1)} %copy-done.11) | copy-start | bytes 405508
  81.9 25.9 %copy-start.16 = (bf16[528,128]{1,0:T(8,128)(2,1)S(1)}, bf16[528,128]{1,0:T(8,128)(2,1)}, u32[]{:S(2)}) copy-start(bf16[528,128]{1,0:T(8,128)(2,1)} %copy-done.14) | copy-start | bytes 405508
  81.9 25.9 %copy-start.19 = (bf16[528,128]{1,0:T(8,128)(2,1)S(1)}, bf16[528,128]{1,0:T(8,128)(2,1)}, u32[]{:S(2)}) copy-start(bf16[528,128]{1,0:T(8,128)(2,1)} %copy-done.17) | copy-start | bytes 405508
  81.9 25.9 %copy-start.22 = (bf16[528,128]{1,0:T(8,128)(2,1)S(1)}, bf16[528,128]{1,0:T(8,128)(2,1)}, u32[]{:S(2)}) copy-start(bf16[528,128]{1,0:T(8,128)(2,1)} %copy-done.20) | copy-start | bytes 405508
  92.7 7.7 %collective-permute-start.32 = (bf16[144,512]{1,0:T(8,128)(2,1)S(1)}, bf16[144,512]{1,0:T(8,128)(2,1)S(1)}, u32[]{:S(2)}, u32[]{:S(2)}) collective-permute-start(bf16[144,512]{1,0:T(8,128)(2,1)S(1)} %get-tuple-element.39.refs_0_), channel_id=1, source_target_pairs={{4,0},{0,4},{12,8},{8,12},{5,1},{1,5},{13,9},{9,13},{6,2},{2,6},{1... | collective-permute-start | bytes 442376 | tf_op jit(solution)/shard_map/ppermute | solution.py:65
  93.8 13.9 %collective-permute-start.33 = (bf16[144,512]{1,0:T(8,128)(2,1)S(1)}, bf16[144,512]{1,0:T(8,128)(2,1)S(1)}, u32[]{:S(2)}, u32[]{:S(2)}) collective-permute-start(bf16[144,512]{1,0:T(8,128)(2,1)S(1)} %get-tuple-element.39.refs_0_), channel_id=1, source_target_pairs={{8,0},{12,4},{0,8},{4,12},{9,1},{13,5},{1,9},{5,13},{10,2},{14,6},... | collective-permute-start | bytes 442376 | tf_op jit(solution)/shard_map/ppermute | solution.py:65
  94.7 13.0 %collective-permute-start.34 = (bf16[144,512]{1,0:T(8,128)(2,1)S(1)}, bf16[144,512]{1,0:T(8,128)(2,1)S(1)}, u32[]{:S(2)}, u32[]{:S(2)}) collective-permute-start(bf16[144,512]{1,0:T(8,128)(2,1)S(1)} %get-tuple-element.39.refs_0_), channel_id=1, source_target_pairs={{12,0},{8,4},{4,8},{0,12},{13,1},{9,5},{5,9},{1,13},{14,2},{10,6},... | collective-permute-start | bytes 442376 | tf_op jit(solution)/shard_map/ppermute | solution.py:65
  100.5 10.5 %collective-permute-start.35 = (f32[64,256]{1,0:T(8,128)S(1)}, f32[64,256]{1,0:T(8,128)S(1)}, u32[]{:S(2)}, u32[]{:S(2)}) collective-permute-start(f32[64,256]{1,0:T(8,128)S(1)} %get-tuple-element.47), channel_id=1, source_target_pairs={{0,1},{1,0},{2,3},{3,2},{4,5},{5,4},{6,7},{7,6},{8,9},{9,8},{10,11... | collective-permute-start | bytes 196616 | tf_op jit(solution)/shard_map/ppermute | solution.py:76
  101.0 9.9 %collective-permute-start.36 = (f32[64,256]{1,0:T(8,128)S(1)}, f32[64,256]{1,0:T(8,128)S(1)}, u32[]{:S(2)}, u32[]{:S(2)}) collective-permute-start(f32[64,256]{1,0:T(8,128)S(1)} %get-tuple-element.48), channel_id=1, source_target_pairs={{0,2},{1,3},{2,0},{3,1},{4,6},{5,7},{6,4},{7,5},{8,10},{9,11},{10,... | collective-permute-start | bytes 196616 | tf_op jit(solution)/shard_map/ppermute | solution.py:76
  101.8 9.2 %collective-permute-start.37 = (f32[64,256]{1,0:T(8,128)S(1)}, f32[64,256]{1,0:T(8,128)S(1)}, u32[]{:S(2)}, u32[]{:S(2)}) collective-permute-start(f32[64,256]{1,0:T(8,128)S(1)} %get-tuple-element.49), channel_id=1, source_target_pairs={{0,3},{1,2},{2,1},{3,0},{4,7},{5,6},{6,5},{7,4},{8,11},{9,10},{10,... | collective-permute-start | bytes 196616 | tf_op jit(solution)/shard_map/ppermute | solution.py:76
  (4 other events, 2.6 us)
